TPU v7x, 32 devices: a whole 2x2x4 slice. The times are simulated.
32 devices in a mesh: az: 8 (over y, x, core), el: 4 (over z).
Axes of the slice: x: 2, y: 2, z: 4, core: 2. Of those that a mesh axis runs over, the one named last changes fastest.
Arguments:
- features: bfloat16 [64, 128, 2048], P(None, 'el', 'az'), may hold values from -30 to 30
- points_xyz: bfloat16 [3, 128, 2048], P(None, 'el', 'az'), may hold values from -4 to 4
- return_mask: int32 [128, 2048], P('el', 'az'), may hold values 0 or 1
- owner_tile: int32 [128, 2048], P('el', 'az'), may hold values from 0 to 31, as said below
- bev_cell: int32 [128, 2048], P('el', 'az'), may hold values from 0 to 2047
- meta_proj: float32 [2, 3, 64], replicated, may hold values from -3.5 to 3.5
- meta_bias: float32 [2, 64], replicated, may hold values from -4 to 4
- conv_weight: bfloat16 [2, 9, 64, 64], replicated, may hold values from -0.25 to 0.25
- norm_gain: float32 [2, 64], replicated, may hold values from 0.25 to 1.75
- head_weight: bfloat16 [9, 64, 128], replicated, may hold values from -0.25 to 0.25
- head_bias: float32 [128], replicated, may hold values from -3 to 3
Outputs:
- head_features: bfloat16 [128, 128, 512], P(None, 'az', 'el')
Inputs may be any that keep to these rules, and one draw needn't show every extreme that they name: `owner_tile`: among the pixels of one elevation band of 32 rows and one azimuth sector of 256 columns, at most 512 name the same tile; in every draw some tile is named exactly 512 times by every such block.
All inputs are finite; a program needn't handle non-finite values. No bound on the sum of `return_mask` on one device may be relied on, other than what follows from the above.
Results may differ from a plain program's by a relative error of at most 0.0054.
Values may be sent and summed in bfloat16 or wider, within the bound.
A program may use at most 64 MiB of HBM per device.

v0:
```python
import jax
import jax.numpy as jnp
from jax import lax
from jax.experimental import pallas as pl
from jax.experimental.pallas import tpu as pltpu
from jax.sharding import PartitionSpec as P

CH = 64
HEAD_CH = 128
TILE_Y = 16
TILE_X = 128
F32 = jnp.float32
BF16 = jnp.bfloat16
WIDE = 144


def padded_2(cells, sides, width, closed):
    for axis, dim in sides:
        count = lax.axis_size(axis)
        ends = count if closed else count - 1
        head = lax.slice_in_dim(cells, 0, width, axis=dim)
        tail = lax.slice_in_dim(cells, cells.shape[dim] - width, cells.shape[dim], axis=dim)
        cells = jnp.concatenate(
            [
                lax.ppermute(tail, axis, [(i, (i + 1) % count) for i in range(ends)]),
                cells,
                lax.ppermute(head, axis, [((i + 1) % count, i) for i in range(ends)]),
            ],
            axis=dim,
        )
    return cells


def slot_ranks(owners, devices):
    count_pts = owners.shape[0]
    group = min(128, count_pts)
    member = (owners[:, None] == jnp.arange(devices, dtype=jnp.int32)[None, :]).astype(BF16)
    blocks = member.reshape(count_pts // group, group, devices)
    lower = (
        lax.broadcasted_iota(jnp.int32, (group, group), 0)
        > lax.broadcasted_iota(jnp.int32, (group, group), 1)
    ).astype(BF16)
    inside = jnp.einsum("ij,bjd->bid", lower, blocks, preferred_element_type=F32)
    totals = jnp.sum(blocks, axis=1, dtype=F32)
    before = jnp.cumsum(totals, axis=0) - totals
    ranks = jnp.sum(jnp.where(blocks > 0, inside + before[:, None, :], 0.0), axis=2)
    return ranks.reshape(-1).astype(jnp.int32)


def layers_kernel(
    height, tiles, cap,
    tgt_ref, xp_ref, aux_ref, waux_ref, bias_ref, gain_ref, conv_ref, mean_ref, lab_ref,
    msg_ref,
    q1, q2, mk, x0, x1, wt, pts, dest,
):
    @pl.loop(0, height + 4)
    def _(r):
        got = jnp.dot(aux_ref[r], waux_ref[...], preferred_element_type=F32)
        q1[r] = got[:, 0:128]
        q2[r] = got[:, 128:256]
        mk[r] = got[:, 256:384]
        x0[r] = xp_ref[r].astype(F32) * (got[:, 256:384] * 0.5)

    def layer(l, rows, width, per, q, x, qrow, qcol, emit):
        @pl.loop(0, rows // per)
        def _(s):
            for u in range(per):
                r = s * per + u
                shift = q[r + 1 + qrow, pl.ds(1 + qcol, width), :] - bias_ref[l : l + 1, :]
                for k in range(9):
                    a, b = k // 3, k % 3
                    arg = q[r + a + qrow, pl.ds(b + qcol, width), :] - shift
                    half = x[r + a, pl.ds(b, width), :]
                    wt[pl.ds(u * width, width), k * 128 : (k + 1) * 128] = (
                        half + half * jnp.tanh(arg)
                    ).astype(BF16)
            y = jnp.dot(wt[0 : per * width, :], conv_ref[l], preferred_element_type=F32)
            ms = jnp.dot((y * y).astype(BF16), mean_ref[...], preferred_element_type=F32)
            act = jnp.maximum(y * lax.rsqrt(ms + 1e-6) * gain_ref[l : l + 1, :], 0.0)
            for u in range(per):
                r = s * per + u
                new = x[r + 1, pl.ds(1, width), :] * 2.0 + act[u * width : (u + 1) * width, :]
                new = new * mk[r + 1 + qrow, pl.ds(1 + qcol, width), :]
                emit(r, new.astype(BF16).astype(F32))

    def emit1(r, new):
        x1[r] = new * 0.5

    def emit2(r, new):
        pts[pl.ds(pl.multiple_of(r * 256, 256), 128), :] = new
        pts[pl.ds(pl.multiple_of(r * 256 + 128, 128), 128), :] = pltpu.roll(new, 64, 1)

    layer(0, height + 2, 136, 2, q1, x0, 0, 0, emit1)
    layer(1, height, 128, 4, q2, x1, 1, 1, emit2)

    unroll = 64

    @pl.loop(0, height * 256 // unroll)
    def _(i):
        base = i * unroll
        for u in range(unroll):
            dest[pl.ds(tgt_ref[base + u], 1), :] = pts[pl.ds(base + u, 1), :]

    left = lax.broadcasted_iota(jnp.int32, (cap // 2, 128), 1) < 64

    @pl.loop(0, tiles)
    def _(t):
        low = dest[pl.ds(pl.multiple_of(t * cap, cap), cap // 2), :]
        high = dest[pl.ds(pl.multiple_of(t * cap + cap // 2, cap // 2), cap // 2), :]
        msg_ref[t, 0 : cap // 2, :] = jnp.where(left, low, pltpu.roll(high, 64, 1)).astype(BF16)
        msg_ref[t, cap // 2 : cap // 2 + 16, :] = lab_ref[t]


def cells_kernel(cap, per, msg_ref, out_ref, acc):
    s = pl.program_id(0)

    @pl.when(s == 0)
    def _():
        acc[...] = jnp.zeros_like(acc)

    half = cap // 2
    size = per * cap
    codes = lax.broadcasted_iota(jnp.int32, (256, 1), 0).astype(F32).astype(BF16)
    his, los, feats = [], [], []
    for p in range(per):
        body = jnp.transpose(msg_ref[p, 0:half, :])
        labels = msg_ref[p, half : half + 16, :]
        lanes = min(cap, 128)
        for j in range(cap // lanes):
            his.append(labels[j : j + 1, 0:lanes])
            los.append(labels[8 + j : 9 + j, 0:lanes])
        feats.append(body[0:64, :])
        feats.append(body[64:128, :])
    hi = jnp.concatenate(his, axis=1)
    lo = jnp.concatenate(los, axis=1)
    feat = jnp.concatenate(feats, axis=1)
    zero = jnp.zeros((64, size), BF16)
    parts = [jnp.where(hi == jnp.array(k, BF16), feat, zero) for k in range(8)]
    marks = lax.broadcasted_iota(jnp.int32, (16, 1), 0).astype(F32).astype(BF16)
    one = jnp.ones((16, size), BF16)
    parts.append(jnp.where(marks == hi, one, jnp.zeros((16, size), BF16)))
    lhs = jnp.concatenate(parts, axis=0)
    rhs = jnp.where(codes == lo, jnp.ones((256, size), BF16), jnp.zeros((256, size), BF16))
    acc[...] += lax.dot_general(
        lhs, rhs, (((1,), (1,)), ((), ())), preferred_element_type=F32
    )

    @pl.when(s == pl.num_programs(0) - 1)
    def _():
        for h in range(8):
            inv = jnp.maximum(acc[512 + h : 513 + h, :], 1.0)
            bev = (acc[h * 64 : (h + 1) * 64, :] / inv).astype(BF16)
            out_ref[2 * h] = bev[:, 0:128]
            out_ref[2 * h + 1] = bev[:, 128:256]


def block_pair(w):
    zero = jnp.zeros_like(w)
    return jnp.concatenate(
        [jnp.concatenate([w, zero], axis=-1), jnp.concatenate([zero, w], axis=-1)], axis=-2
    )


def on_device(
    features, points_xyz, return_mask, owner_tile, bev_cell,
    meta_proj, meta_bias, conv_weight, norm_gain, head_weight, head_bias,
):
    height, breadth = return_mask.shape
    az_count = lax.axis_size("az")
    el_count = lax.axis_size("el")
    devices = az_count * el_count
    count_pts = height * breadth
    cap = 2 * count_pts // devices

    stacked = jnp.concatenate([features, points_xyz, return_mask.astype(BF16)[None]], axis=0)
    stacked = padded_2(stacked, (("az", 2),), 2, True)
    stacked = padded_2(stacked, (("el", 1),), 2, False)
    turned = stacked.transpose(1, 2, 0)
    first, last = turned[:, 0:132], turned[:, 128:260]
    grow = ((0, 0), (0, WIDE - 132), (0, 0))
    xp = jnp.pad(jnp.concatenate([first[..., :CH], last[..., :CH]], axis=2), grow)
    spots = jnp.concatenate([first[..., CH:], last[..., CH:]], axis=2)
    aux = jnp.pad(
        jnp.concatenate([spots, spots, spots], axis=2), ((0, 0), (0, WIDE - 132), (0, 8))
    )

    proj = meta_proj * 0.5
    top = lax.reduce_precision(proj, 8, 7)
    mid = lax.reduce_precision(proj - top, 8, 7)
    low = lax.reduce_precision(proj - top - mid, 8, 7)
    rows = []
    for i, part in enumerate((top, mid, low)):
        flag = jnp.full((1, CH), 1.0 if i == 0 else 0.0, F32)
        nil3, nil1 = jnp.zeros((3, CH), F32), jnp.zeros((1, CH), F32)
        wide = [
            block_pair(jnp.concatenate([part[0], nil1], axis=0)),
            block_pair(jnp.concatenate([part[1], nil1], axis=0)),
            block_pair(jnp.concatenate([nil3, flag], axis=0)),
        ]
        rows.append(jnp.concatenate(wide, axis=1))
    waux = jnp.pad(jnp.concatenate(rows, axis=0), ((0, 8), (0, 0))).astype(BF16)
    bias = jnp.concatenate([meta_bias, meta_bias], axis=1) * 0.5
    gain = jnp.concatenate([norm_gain, norm_gain], axis=1)
    conv = block_pair(conv_weight).reshape(2, 9 * 128, 128)
    mean = block_pair(jnp.full((CH, CH), 1.0 / CH, BF16))

    owners = owner_tile.reshape(-1)
    cells = bev_cell.reshape(-1)
    keep = return_mask.reshape(-1)
    ranks = slot_ranks(owners, devices)
    target = owners * cap + ranks
    member = owners[None, :] == jnp.arange(devices, dtype=jnp.int32)[:, None]
    hi = jnp.where(keep > 0, cells // 256 + 1, 0)
    lo = jnp.where(keep > 0, cells % 256 + 1, 0)
    value = jnp.stack([hi, lo], axis=0).astype(BF16)
    left = jnp.where(member[None], value[:, None, :], 0).astype(BF16)
    right = (ranks[:, None] == jnp.arange(cap, dtype=jnp.int32)[None, :]).astype(BF16)
    labels = jnp.einsum("vtp,pr->tvr", left, right, preferred_element_type=F32) - 1.0
    lanes = min(cap, 128)
    labels = labels.reshape(devices, 2, cap // lanes, lanes)
    labels = jnp.pad(
        labels, ((0, 0), (0, 0), (0, 8 - cap // lanes), (0, 128 - lanes))
    ).reshape(devices, 16, 128).astype(BF16)

    vm = pl.BlockSpec(memory_space=pltpu.VMEM)
    deep = cap // 2 + 16
    plane = pltpu.VMEM((height + 4, WIDE, 128), F32)
    msg = pl.pallas_call(
        lambda *refs: layers_kernel(height, devices, cap, *refs),
        out_shape=jax.ShapeDtypeStruct((devices, deep, 128), BF16),
        in_specs=[pl.BlockSpec(memory_space=pltpu.SMEM)] + [vm] * 8,
        out_specs=vm,
        scratch_shapes=[
            plane, plane, plane, plane,
            pltpu.VMEM((height + 2, 136, 128), F32),
            pltpu.VMEM((512, 9 * 128), BF16),
            pltpu.VMEM((count_pts, 128), F32),
            pltpu.VMEM((devices * cap, 128), F32),
        ],
        compiler_params=pltpu.CompilerParams(vmem_limit_bytes=56 << 20),
        name="layers",
    )(target, xp, aux, waux, bias, gain, conv, mean, labels)

    got = lax.all_to_all(msg, ("az", "el"), split_axis=0, concat_axis=0, tiled=True)

    per = max(1, 512 // cap)
    grid = pl.pallas_call(
        lambda *refs: cells_kernel(cap, per, *refs),
        out_shape=jax.ShapeDtypeStruct((TILE_Y, CH, TILE_X), BF16),
        grid=(devices // per,),
        in_specs=[pl.BlockSpec((per, deep, 128), lambda s: (s, 0, 0))],
        out_specs=pl.BlockSpec((TILE_Y, CH, TILE_X), lambda s: (0, 0, 0)),
        scratch_shapes=[pltpu.VMEM((528, 256), F32)],
        compiler_params=pltpu.CompilerParams(vmem_limit_bytes=56 << 20),
        name="cells",
    )(got)

    framed = padded_2(grid, (("az", 0), ("el", 2)), 1, False)
    summed = jnp.zeros((HEAD_CH, TILE_Y, TILE_X), F32)
    for k in range(9):
        a = k // 3
        b = k % 3
        summed = summed + jnp.einsum(
            "cd,hcw->dhw",
            head_weight[k],
            framed[a : a + TILE_Y, :, b : b + TILE_X],
            preferred_element_type=F32,
        )
    return jnp.maximum(summed + head_bias[:, None, None], 0.0).astype(BF16)


def solution(mesh):
    placed = (
        P(None, "el", "az"),
        P(None, "el", "az"),
        P("el", "az"),
        P("el", "az"),
        P("el", "az"),
        P(),
        P(),
        P(),
        P(),
        P(),
        P(),
    )
    return jax.shard_map(
        on_device, mesh=mesh, in_specs=placed, out_specs=P(None, "az", "el"), check_vma=False
    )
```

profile of v0, /device:TPU:0, one launch (start us, length us, event | category | flops | bytes accessed | tf_op | source)
XLA Modules:
  0.0 189.0 jit_solution(6113730734452691847)
XLA Ops:
  0.0 0.9 convert_bitcast_fusion.1
  0.9 1.0 copy.38
  1.9 0.0 copy-start.10
  1.9 2.2 %copy.36 = bf16[64,32,256]{0,2,1:T(8,128)(2,1)} copy(bf16[64,32,256]{2,1,0:T(8,128)(2,1)S(1)} %copy-done.5) | data formatting | bytes 2097152 | tf_op args[0]
  4.1 1.8 copy.37
  6.0 1.1 pad_maximum_fusion.10
  7.1 0.0 copy-start.12
  7.1 0.0 copy-start.11
  7.1 0.5 collective-permute-start
  7.6 2.9 %collective-permute-start.1 = (bf16[68,32,2]{0,2,1:T(2,128)(2,1)S(1)}, bf16[68,32,2]{0,2,1:T(2,128)(2,1)S(1)}, u32[]{:S(2)}, u32[]{:S(2)}) collective-permute-start(bf16[68,32,2]{0,2,1:T(2,128)(2,1)S(1)} %get-tuple-element.8), channel_id=1, source_target_pairs={{4,0},{8,4},{12,8},{16,12},{20,16},{24,20},{28,24},{0,28},{5,1},{9... | collective-permute-start | bytes 26120 | tf_op jit(solution)/shard_map/ppermute | solution.py:27
  10.6 0.3 convert_reduce_fusion
  10.9 0.1 reduce_window_sum.11
  11.0 0.5 fusion.18
  11.6 0.1 iota_compare_fusion.4
  11.7 0.6 multiply_add_fusion.refs_0_
  12.5 0.3 select_convert_fusion
  12.8 0.1 pad_maximum_fusion.7
  12.9 0.0 copy-start.6
  12.9 0.0 copy-start.13
  13.0 2.8 %fusion.28 = bf16[32,2,512]{2,0,1:T(8,128)(2,1)S(1)} fusion(s32[8192]{0:T(1024)S(1)} %convert_bitcast_fusion, pred[32,8192]{1,0:T(8,128)(4,1)S(1)} %iota_compare_fusion.4, bf16[2,8192]{1,0:T(2,128)(2,1)S(1)} %pad_maximum_fusion.7), kind=kOutput, calls=%fused_computation.31 | convolution fusion | flops 541655040 | bytes 393216 | tf_op jit(solution)/shard_map/vtp,pr->tvr/dot_general | solution.py:218
  15.8 0.7 pad_bitcast_fusion.refs_8_
  16.5 1.0 fusion.34
  17.5 0.1 fusion.102
  17.6 0.6 pad.52.refs_3_
  18.2 0.0 collective-permute-done
  18.2 0.0 collective-permute-done.1
  18.2 1.6 pad_maximum_fusion.6
  19.8 4.2 %collective-permute-start.2 = (bf16[68,2,260]{0,2,1:T(8,128)(2,1)S(1)}, bf16[68,2,260]{0,2,1:T(8,128)(2,1)S(1)}, u32[]{:S(2)}, u32[]{:S(2)}) collective-permute-start(bf16[68,2,260]{0,2,1:T(8,128)(2,1)S(1)} %get-tuple-element.5), channel_id=1, source_target_pairs={{0,1},{1,2},{2,3},{4,5},{5,6},{6,7},{8,9},{9,10},{10,11},{12,13},{... | collective-permute-start | bytes 212168 | tf_op jit(solution)/shard_map/ppermute | solution.py:25
  24.0 1.5 collective-permute-start.3
  25.5 0.7 maximum_multiply_fusion
  26.2 0.4 collective-permute-done.2
  26.6 4.4 %collective-permute-done.3 = bf16[68,2,260]{0,2,1:T(8,128)(2,1)S(1)} collective-permute-done((bf16[68,2,260]{0,2,1:T(8,128)(2,1)S(1)}, bf16[68,2,260]{0,2,1:T(8,128)(2,1)S(1)}, u32[]{:S(2)}, u32[]{:S(2)}) %collective-permute-start.3) | collective-permute-done | bytes 70752 | tf_op jit(solution)/shard_map/ppermute | solution.py:27
  30.9 5.7 %maximum_bitcast_fusion = bf16[36,260,68]{2,1,0:T(8,128)(2,1)S(1)} fusion(bf16[68,2,260]{0,2,1:T(8,128)(2,1)S(1)} %collective-permute-done.3, bf16[68,32,2]{0,2,1:T(2,128)(2,1)S(1)} %collective-permute-done.1, bf16[1,32,256]{0,2,1:T(8,128)(2,1)S(1)} %copy.38, bf16[3,32,256]{0,2,1:T(8,128)(2,1)S(1)} %copy-done.1, bf16[64,32,256]{0,2,1:T(8,128)(2,1)S(1)} %copy-done, ...), kind=kLoop, calls=%fused_computation.7 | loop fusion | flops 8910720 | bytes 2545920 | tf_op jit(solution)/shard_map/transpose | solution.py:178
  36.7 0.7 fusion.146
  37.4 1.6 fusion.147
  39.1 5.1 %concatenate.155 = bf16[36,132,24]{2,1,0:T(8,128)(2,1)} concatenate(bf16[36,132,4]{2,1,0:T(8,128)(2,1)S(1)} %get-tuple-element.10, bf16[36,132,4]{2,1,0:T(8,128)(2,1)S(1)} %get-tuple-element.9, bf16[36,132,4]{2,1,0:T(8,128)(2,1)S(1)} %get-tuple-element.10, bf16[36,132,4]{2,1,0:T(8,128)(2,1)S(1)} %get-tuple-element.9, bf16[36,132,4]{2,1,0:T(8,128)(2,1)S(1)} %get-tuple-element.10, ...), dimensions={2} | concatenate | bytes 456192 | tf_op jit(solution)/shard_map/concatenate | solution.py:184
  44.1 2.8 %pad.51.refs_2_ = bf16[36,144,32]{2,1,0:T(8,128)(2,1)} pad(bf16[36,132,24]{2,1,0:T(8,128)(2,1)} %concatenate.155, bf16[]{:T(256)} %constant.47.clone.1), padding=0_0x0_12x0_8 | pad | bytes 559874 | tf_op jit(solution)/shard_map/jit(_pad)/pad | solution.py:183
  46.9 1.8 fusion.16.refs_1_
  48.8 37.2 %layers.1 = bf16[32,272,128]{2,1,0:T(8,128)(2,1)} custom-call(s32[8192]{0:T(1024)} %multiply_add_fusion.refs_0_, bf16[36,144,128]{2,1,0:T(8,128)(2,1)} %fusion.16.refs_1_, bf16[36,144,32]{2,1,0:T(8,128)(2,1)} %pad.51.refs_2_, bf16[32,384]{1,0:T(8,128)(2,1)} %pad.52.refs_3_, f32[2,128]{1,0:T(2,128)} %get-tuple-element.34.refs_4_, ...), custom_call_target="tpu_custom_call" | custom-call | tf_op jit(solution)/shard_map/layers/pallas_call | solution.py:228
  86.0 56.6 %all_to_all.5.refs_0_ = bf16[32,272,128]{2,1,0:T(8,128)(2,1)} all-to-all(bf16[32,272,128]{2,1,0:T(8,128)(2,1)} %layers.1), channel_id=1, replica_groups=mesh['az'=8,'el'=4] {'az','el'}, dimensions={0} | all-to-all | bytes 4456448 | tf_op jit(solution)/shard_map/all_to_all | solution.py:244
  142.6 21.1 %cells.1 = bf16[16,64,128]{2,1,0:T(8,128)(2,1)} custom-call(bf16[32,272,128]{2,1,0:T(8,128)(2,1)} %all_to_all.5.refs_0_), custom_call_target="tpu_custom_call" | custom-call | tf_op jit(solution)/shard_map/cells/pallas_call | solution.py:247
  163.8 0.8 fusion.149
  164.6 2.3 %collective-permute-start.4 = (bf16[1,64,128]{2,1,0:T(8,128)(2,1)S(1)}, bf16[1,64,128]{2,1,0:T(8,128)(2,1)S(1)}, u32[]{:S(2)}, u32[]{:S(2)}) collective-permute-start(bf16[1,64,128]{2,1,0:T(8,128)(2,1)S(1)} %get-tuple-element.17), channel_id=1, source_target_pairs={{0,4},{4,8},{8,12},{12,16},{16,20},{20,24},{24,28},{1,5},{5,9},{9,... | collective-permute-start | bytes 49160 | tf_op jit(solution)/shard_map/ppermute | solution.py:25
  166.8 1.3 collective-permute-start.5
  168.2 1.3 fusion.125
  169.5 0.6 collective-permute-done.5
  170.1 1.0 pad_maximum_fusion.1
  171.0 0.2 fusion.148
  171.2 2.8 %collective-permute-start.6 = (bf16[18,64,1]{2,1,0:T(8,128)(2,1)S(1)}, bf16[18,64,1]{2,1,0:T(8,128)(2,1)S(1)}, u32[]{:S(2)}, u32[]{:S(2)}) collective-permute-start(bf16[18,64,1]{2,1,0:T(8,128)(2,1)S(1)} %get-tuple-element.15), channel_id=1, source_target_pairs={{0,1},{1,2},{2,3},{4,5},{5,6},{6,7},{8,9},{9,10},{10,11},{12,13},{... | collective-permute-start | bytes 6920 | tf_op jit(solution)/shard_map/ppermute | solution.py:25
  174.0 1.3 collective-permute-start.7
  175.3 0.3 fusion.38
  175.6 0.3 fusion.42
  175.9 3.8 %collective-permute-done.6 = bf16[18,64,1]{2,1,0:T(8,128)(2,1)S(1)} collective-permute-done((bf16[18,64,1]{2,1,0:T(8,128)(2,1)S(1)}, bf16[18,64,1]{2,1,0:T(8,128)(2,1)S(1)}, u32[]{:S(2)}, u32[]{:S(2)}) %collective-permute-start.6) | collective-permute-done | bytes 2336 | tf_op jit(solution)/shard_map/ppermute | solution.py:25
  179.8 4.7 %collective-permute-done.7 = bf16[18,64,1]{2,1,0:T(8,128)(2,1)S(1)} collective-permute-done((bf16[18,64,1]{2,1,0:T(8,128)(2,1)S(1)}, bf16[18,64,1]{2,1,0:T(8,128)(2,1)S(1)}, u32[]{:S(2)}, u32[]{:S(2)}) %collective-permute-start.7) | collective-permute-done | bytes 2336 | tf_op jit(solution)/shard_map/ppermute | solution.py:27
  184.5 0.4 maximum_maximum_fusion
  184.9 0.5 fusion.53
  185.4 0.5 fusion.46
  185.9 0.3 fusion.51
  186.2 0.3 fusion.48
  186.5 0.0 copy-start.16
  186.6 0.5 fusion.13
  187.0 0.2 copy-done.16
  187.2 0.6 fusion.19
  187.8 1.2 copy.41
  (45 shorter events, 0.2 us)
Async XLA Ops:
  0.0 1.9 %copy-start.5 = (bf16[64,32,256]{2,1,0:T(8,128)(2,1)S(1)}, bf16[64,32,256]{2,1,0:T(8,128)(2,1)}, u32[]{:S(2)}) copy-start(bf16[64,32,256]{2,1,0:T(8,128)(2,1)} %param.11) | copy-start | bytes 3145732
  1.9 2.2 %copy-start.10 = (bf16[3,32,256]{2,1,0:T(8,128)(2,1)S(1)}, bf16[3,32,256]{2,1,0:T(8,128)(2,1)}, u32[]{:S(2)}) copy-start(bf16[3,32,256]{2,1,0:T(8,128)(2,1)} %param.12) | copy-start | bytes 147460
  6.0 4.6 %copy-start.8 = (s32[32,256]{1,0:T(8,128)S(1)}, s32[32,256]{1,0:T(8,128)}, u32[]{:S(2)}) copy-start(s32[32,256]{1,0:T(8,128)} %param.13) | copy-start | bytes 98308
  6.0 4.6 %copy-start.9 = (s32[32,256]{1,0:T(8,128)S(1)}, s32[32,256]{1,0:T(8,128)}, u32[]{:S(2)}) copy-start(s32[32,256]{1,0:T(8,128)} %param.14) | copy-start | bytes 98308
  7.1 5.3 %copy-start.12 = (f32[2,3,64]{2,0,1:T(2,128)S(1)}, f32[2,3,64]{2,0,1:T(2,128)}, u32[]{:S(2)}) copy-start(f32[2,3,64]{2,0,1:T(2,128)} %param.16) | copy-start | bytes 4612
  7.1 5.4 %copy-start.11 = (s32[32,256]{1,0:T(8,128)S(1)}, s32[32,256]{1,0:T(8,128)}, u32[]{:S(2)}) copy-start(s32[32,256]{1,0:T(8,128)} %param.15) | copy-start | bytes 98308
  7.1 11.1 %collective-permute-start = (bf16[68,32,2]{0,2,1:T(2,128)(2,1)S(1)}, bf16[68,32,2]{0,2,1:T(2,128)(2,1)S(1)}, u32[]{:S(2)}, u32[]{:S(2)}) collective-permute-start(bf16[68,32,2]{0,2,1:T(2,128)(2,1)S(1)} %get-tuple-element.7), channel_id=1, source_target_pairs={{0,4},{4,8},{8,12},{12,16},{16,20},{20,24},{24,28},{28,0},{1,5},{5... | collective-permute-start | bytes 26120 | tf_op jit(solution)/shard_map/ppermute | solution.py:25
  7.6 10.6 %collective-permute-start.1 = (bf16[68,32,2]{0,2,1:T(2,128)(2,1)S(1)}, bf16[68,32,2]{0,2,1:T(2,128)(2,1)S(1)}, u32[]{:S(2)}, u32[]{:S(2)}) collective-permute-start(bf16[68,32,2]{0,2,1:T(2,128)(2,1)S(1)} %get-tuple-element.8), channel_id=1, source_target_pairs={{4,0},{8,4},{12,8},{16,12},{20,16},{24,20},{28,24},{0,28},{5,1},{9... | collective-permute-start | bytes 26120 | tf_op jit(solution)/shard_map/ppermute | solution.py:27
  12.9 3.5 %copy-start.6 = (bf16[2,9,64,64]{3,2,1,0:T(8,128)(2,1)S(1)}, bf16[2,9,64,64]{3,2,1,0:T(8,128)(2,1)}, u32[]{:S(2)}) copy-start(bf16[2,9,64,64]{3,2,1,0:T(8,128)(2,1)} %param.18) | copy-start | bytes 442372
  12.9 4.5 %copy-start.13 = (bf16[8,128]{1,0:T(8,128)(2,1)S(1)}, bf16[8,128]{1,0:T(8,128)(2,1)}, u32[]{:S(2)}) copy-start(bf16[8,128]{1,0:T(8,128)(2,1)} %constant.50.clone.1) | copy-start | bytes 6148
  18.2 7.3 %copy-start.14 = (f32[2,64]{1,0:T(2,128)S(1)}, f32[2,64]{1,0:T(2,128)}, u32[]{:S(2)}) copy-start(f32[2,64]{1,0:T(2,128)} %param.17) | copy-start | bytes 1540
  18.2 7.3 %copy-start.15 = (f32[2,64]{1,0:T(2,128)S(1)}, f32[2,64]{1,0:T(2,128)}, u32[]{:S(2)}) copy-start(f32[2,64]{1,0:T(2,128)} %param.19) | copy-start | bytes 1540
  18.2 12.7 %copy-start = (bf16[64,32,256]{0,2,1:T(8,128)(2,1)S(1)}, bf16[64,32,256]{0,2,1:T(8,128)(2,1)}, u32[]{:S(2)}) copy-start(bf16[64,32,256]{0,2,1:T(8,128)(2,1)} %copy.36) | copy-start | bytes 3145732
  18.2 12.7 %copy-start.1 = (bf16[3,32,256]{0,2,1:T(8,128)(2,1)S(1)}, bf16[3,32,256]{0,2,1:T(8,128)(2,1)}, u32[]{:S(2)}) copy-start(bf16[3,32,256]{0,2,1:T(8,128)(2,1)} %copy.37) | copy-start | bytes 147460
  19.8 6.7 %collective-permute-start.2 = (bf16[68,2,260]{0,2,1:T(8,128)(2,1)S(1)}, bf16[68,2,260]{0,2,1:T(8,128)(2,1)S(1)}, u32[]{:S(2)}, u32[]{:S(2)}) collective-permute-start(bf16[68,2,260]{0,2,1:T(8,128)(2,1)S(1)} %get-tuple-element.5), channel_id=1, source_target_pairs={{0,1},{1,2},{2,3},{4,5},{5,6},{6,7},{8,9},{9,10},{10,11},{12,13},{... | collective-permute-start | bytes 212168 | tf_op jit(solution)/shard_map/ppermute | solution.py:25
  24.0 6.9 %collective-permute-start.3 = (bf16[68,2,260]{0,2,1:T(8,128)(2,1)S(1)}, bf16[68,2,260]{0,2,1:T(8,128)(2,1)S(1)}, u32[]{:S(2)}, u32[]{:S(2)}) collective-permute-start(bf16[68,2,260]{0,2,1:T(8,128)(2,1)S(1)} %get-tuple-element.6), channel_id=1, source_target_pairs={{1,0},{2,1},{3,2},{5,4},{6,5},{7,6},{9,8},{10,9},{11,10},{13,12},{... | collective-permute-start | bytes 212168 | tf_op jit(solution)/shard_map/ppermute | solution.py:27
  44.1 2.8 %copy-start.3 = (bf16[36,132,64]{2,1,0:T(8,128)(2,1)S(1)}, bf16[36,132,64]{2,1,0:T(8,128)(2,1)}, u32[]{:S(2)}) copy-start(bf16[36,132,64]{2,1,0:T(8,128)(2,1)} %get-tuple-element.11) | copy-start | bytes 1824772
  44.1 2.8 %copy-start.4 = (bf16[36,132,64]{2,1,0:T(8,128)(2,1)S(1)}, bf16[36,132,64]{2,1,0:T(8,128)(2,1)}, u32[]{:S(2)}) copy-start(bf16[36,132,64]{2,1,0:T(8,128)(2,1)} %get-tuple-element.12) | copy-start | bytes 1824772
  142.6 25.5 %copy-start.7 = (bf16[9,64,128]{2,1,0:T(8,128)(2,1)S(1)}, bf16[9,64,128]{2,1,0:T(8,128)(2,1)}, u32[]{:S(2)}) copy-start(bf16[9,64,128]{2,1,0:T(8,128)(2,1)} %param.20) | copy-start | bytes 442372
  163.8 11.5 %copy-start.2 = (bf16[16,64,128]{2,1,0:T(8,128)(2,1)S(1)}, bf16[16,64,128]{2,1,0:T(8,128)(2,1)}, u32[]{:S(2)}) copy-start(bf16[16,64,128]{2,1,0:T(8,128)(2,1)} %cells.1) | copy-start | bytes 786436
  164.6 4.9 %collective-permute-start.4 = (bf16[1,64,128]{2,1,0:T(8,128)(2,1)S(1)}, bf16[1,64,128]{2,1,0:T(8,128)(2,1)S(1)}, u32[]{:S(2)}, u32[]{:S(2)}) collective-permute-start(bf16[1,64,128]{2,1,0:T(8,128)(2,1)S(1)} %get-tuple-element.17), channel_id=1, source_target_pairs={{0,4},{4,8},{8,12},{12,16},{16,20},{20,24},{24,28},{1,5},{5,9},{9,... | collective-permute-start | bytes 49160 | tf_op jit(solution)/shard_map/ppermute | solution.py:25
  166.8 3.2 %collective-permute-start.5 = (bf16[1,64,128]{2,1,0:T(8,128)(2,1)S(1)}, bf16[1,64,128]{2,1,0:T(8,128)(2,1)S(1)}, u32[]{:S(2)}, u32[]{:S(2)}) collective-permute-start(bf16[1,64,128]{2,1,0:T(8,128)(2,1)S(1)} %get-tuple-element.18), channel_id=1, source_target_pairs={{4,0},{8,4},{12,8},{16,12},{20,16},{24,20},{28,24},{5,1},{9,5},{13... | collective-permute-start | bytes 49160 | tf_op jit(solution)/shard_map/ppermute | solution.py:27
  171.2 8.5 %collective-permute-start.6 = (bf16[18,64,1]{2,1,0:T(8,128)(2,1)S(1)}, bf16[18,64,1]{2,1,0:T(8,128)(2,1)S(1)}, u32[]{:S(2)}, u32[]{:S(2)}) collective-permute-start(bf16[18,64,1]{2,1,0:T(8,128)(2,1)S(1)} %get-tuple-element.15), channel_id=1, source_target_pairs={{0,1},{1,2},{2,3},{4,5},{5,6},{6,7},{8,9},{9,10},{10,11},{12,13},{... | collective-permute-start | bytes 6920 | tf_op jit(solution)/shard_map/ppermute | solution.py:25
  174.0 10.5 %collective-permute-start.7 = (bf16[18,64,1]{2,1,0:T(8,128)(2,1)S(1)}, bf16[18,64,1]{2,1,0:T(8,128)(2,1)S(1)}, u32[]{:S(2)}, u32[]{:S(2)}) collective-permute-start(bf16[18,64,1]{2,1,0:T(8,128)(2,1)S(1)} %get-tuple-element.16), channel_id=1, source_target_pairs={{1,0},{2,1},{3,2},{5,4},{6,5},{7,6},{9,8},{10,9},{11,10},{13,12},{... | collective-permute-start | bytes 6920 | tf_op jit(solution)/shard_map/ppermute | solution.py:27
  186.5 0.7 copy-start.16
where the time goes:
time: 191 us; the launch traced here: 189 us
  Pallas kernels  58.4 us (31%)
  blocking collectives  56.6 us (30%)
  local copies, waits for them, and re-layouts  19.2 us (10%)
  starting transfers between devices  16.7 us (9%)
  other arithmetic  15.9 us (8%)
  waiting for transfers between devices  13.9 us (7%)
  matrix products  7.89 us (4%)
    all_to_all x1, blocking collectives, on_device(): lax.all_to_all(msg, ('az', 'el'), split_axis=0, concat_axis=0, tiled=True)  56.6 us
    pallas_call x1, Pallas kernels, on_device(): pl.pallas_call(lambda *refs: layers_kernel(height, devices, cap, *refs),...  37.2 us
    pallas_call x1, Pallas kernels, on_device(): pl.pallas_call(lambda *refs: cells_kernel(cap, per, *refs), out_shape=jax...  21.1 us
    ppermute x4, waiting for transfers between devices, padded_2(): lax.ppermute(head, axis, [((i + 1) % count, i) for i in range(ends)])  9.7 us
    ppermute x4, starting transfers between devices, padded_2(): lax.ppermute(tail, axis, [(i, (i + 1) % count) for i in range(ends)])  9.68 us
    ppermute x4, starting transfers between devices, padded_2(): lax.ppermute(head, axis, [((i + 1) % count, i) for i in range(ends)])  7 us
    transpose x1, other arithmetic, on_device(): turned = stacked.transpose(1, 2, 0)  5.74 us
    concatenate x1, local copies, waits for them, and re-layouts, on_device(): jnp.concatenate([spots, spots, spots], axis=2)  5.06 us
  transfers between devices with their start and end apart: 8, of which 5 were waited for; matrix products, arithmetic and copies ran while one was open for 5% of the time, Pallas kernels for 0%

commit v1 on v0

v1 whole, which is shorter than its diff:
```python
import jax
import jax.numpy as jnp
from jax import lax
from jax.experimental import pallas as pl
from jax.experimental.pallas import tpu as pltpu
from jax.sharding import PartitionSpec as P

CH = 64
HEAD_CH = 128
TILE_Y = 16
TILE_X = 128
F32 = jnp.float32
BF16 = jnp.bfloat16
WIDE = 144


def slot_ranks(owners, devices):
    count_pts = owners.shape[0]
    group = min(128, count_pts)
    member = (owners[:, None] == jnp.arange(devices, dtype=jnp.int32)[None, :]).astype(BF16)
    blocks = member.reshape(count_pts // group, group, devices)
    lower = (
        lax.broadcasted_iota(jnp.int32, (group, group), 0)
        > lax.broadcasted_iota(jnp.int32, (group, group), 1)
    ).astype(BF16)
    inside = jnp.einsum("ij,bjd->bid", lower, blocks, preferred_element_type=F32)
    totals = jnp.sum(blocks, axis=1, dtype=F32)
    before = jnp.cumsum(totals, axis=0) - totals
    ranks = jnp.sum(jnp.where(blocks > 0, inside + before[:, None, :], 0.0), axis=2)
    return ranks.reshape(-1).astype(jnp.int32)


def layers_kernel(
    height, tiles, cap,
    tgt_ref, main_ref, left_ref, right_ref, top_ref, low_ref,
    waux_ref, bias_ref, gain_ref, conv_ref, mean_ref, lab_ref,
    msg_ref,
    q1, q2, mk, x0, x1, wt, pts, dest, line,
):
    line[...] = jnp.zeros_like(line)

    def place(slot, r):
        pair = jnp.concatenate(
            [line[slot, 0:WIDE, :].astype(BF16), line[slot, 128 : 128 + WIDE, :].astype(BF16)],
            axis=1,
        )
        got = jnp.dot(pair, waux_ref[...], preferred_element_type=F32)
        q1[r] = got[:, 0:128]
        q2[r] = got[:, 128:256]
        mk[r] = got[:, 256:384]
        x0[r] = got[:, 384:512] * (got[:, 256:384] * 0.5)

    for r in range(2):
        line[r, 0:260, :] = top_ref[r].astype(F32)
        place(r, r)
    for r in range(2):
        line[r, 0:260, :] = low_ref[r].astype(F32)
        place(r, height + 2 + r)

    @pl.loop(0, height // 2)
    def _(s):
        for u in range(2):
            r = s * 2 + u
            line[u, 0:2, :] = left_ref[r].astype(F32)
            line[u, 2:258, :] = main_ref[r].astype(F32)
            line[u, 258:260, :] = right_ref[r].astype(F32)
            place(u, r + 2)

    def layer(l, rows, width, per, q, x, qrow, qcol, emit):
        @pl.loop(0, rows // per)
        def _(s):
            for u in range(per):
                r = s * per + u
                shift = q[r + 1 + qrow, pl.ds(1 + qcol, width), :] - bias_ref[l : l + 1, :]
                for k in range(9):
                    a, b = k // 3, k % 3
                    arg = q[r + a + qrow, pl.ds(b + qcol, width), :] - shift
                    half = x[r + a, pl.ds(b, width), :]
                    wt[pl.ds(u * width, width), k * 128 : (k + 1) * 128] = (
                        half + half * jnp.tanh(arg)
                    ).astype(BF16)
            y = jnp.dot(wt[0 : per * width, :], conv_ref[l], preferred_element_type=F32)
            ms = jnp.dot((y * y).astype(BF16), mean_ref[...], preferred_element_type=F32)
            act = jnp.maximum(y * lax.rsqrt(ms + 1e-6) * gain_ref[l : l + 1, :], 0.0)
            for u in range(per):
                r = s * per + u
                new = x[r + 1, pl.ds(1, width), :] * 2.0 + act[u * width : (u + 1) * width, :]
                new = new * mk[r + 1 + qrow, pl.ds(1 + qcol, width), :]
                emit(r, new.astype(BF16).astype(F32))

    def emit1(r, new):
        x1[r] = new * 0.5

    def emit2(r, new):
        pts[pl.ds(pl.multiple_of(r * 256, 256), 128), :] = new
        pts[pl.ds(pl.multiple_of(r * 256 + 128, 128), 128), :] = pltpu.roll(new, 64, 1)

    layer(0, height + 2, 136, 2, q1, x0, 0, 0, emit1)
    layer(1, height, 128, 4, q2, x1, 1, 1, emit2)

    unroll = 64

    @pl.loop(0, height * 256 // unroll)
    def _(i):
        base = i * unroll
        for u in range(unroll):
            dest[pl.ds(tgt_ref[base + u], 1), :] = pts[pl.ds(base + u, 1), :]

    left = lax.broadcasted_iota(jnp.int32, (cap // 2, 128), 1) < 64

    @pl.loop(0, tiles)
    def _(t):
        low = dest[pl.ds(pl.multiple_of(t * cap, cap), cap // 2), :]
        high = dest[pl.ds(pl.multiple_of(t * cap + cap // 2, cap // 2), cap // 2), :]
        msg_ref[t, 0 : cap // 2, :] = jnp.where(left, low, pltpu.roll(high, 64, 1)).astype(BF16)
        msg_ref[t, cap // 2 : cap // 2 + 16, :] = lab_ref[t]


def cells_kernel(
    cap, az_count, el_count,
    msg_ref, head_ref, bias_ref,
    out_ref,
    got, acc, bev, edges, rims, ends, views,
    send_sem, recv_sem, rim_send, rim_recv,
):
    az, el = lax.axis_index("az"), lax.axis_index("el")
    devices = az_count * el_count
    me = az * el_count + el
    mesh_id = pl.DeviceIdType.MESH

    barrier = pltpu.get_barrier_semaphore()

    def spot(d):
        other = lax.rem(me + d, devices)
        return other, (other // el_count, lax.rem(other, el_count))

    @pl.loop(1, devices)
    def _(d):
        pl.semaphore_signal(barrier, inc=1, device_id=spot(d)[1], device_id_type=mesh_id)

    pl.semaphore_wait(barrier, devices - 1)

    def message(d):
        other, where = spot(d)
        return pltpu.make_async_remote_copy(
            src_ref=msg_ref.at[other],
            dst_ref=got.at[d],
            send_sem=send_sem.at[d],
            recv_sem=recv_sem.at[d],
            device_id=where,
            device_id_type=mesh_id,
        )

    @pl.loop(1, devices)
    def _(d):
        message(d).start()

    half = cap // 2
    lanes = min(cap, 128)
    codes = lax.broadcasted_iota(jnp.int32, (256, 1), 0).astype(F32).astype(BF16)
    marks = lax.broadcasted_iota(jnp.int32, (16, 1), 0).astype(F32).astype(BF16)
    zero = jnp.zeros((64, cap), BF16)

    def add(block, labels):
        body = jnp.transpose(block)
        count = cap // lanes
        hi = jnp.concatenate([labels[j : j + 1, 0:lanes] for j in range(count)], axis=1)
        lo = jnp.concatenate([labels[8 + j : 9 + j, 0:lanes] for j in range(count)], axis=1)
        feat = jnp.concatenate([body[0:64, :], body[64:128, :]], axis=1)
        parts = [jnp.where(hi == jnp.array(k, BF16), feat, zero) for k in range(8)]
        parts.append(
            jnp.where(marks == hi, jnp.ones((16, cap), BF16), jnp.zeros((16, cap), BF16))
        )
        rhs = jnp.where(codes == lo, jnp.ones((256, cap), BF16), jnp.zeros((256, cap), BF16))
        return lax.dot_general(
            jnp.concatenate(parts, axis=0), rhs, (((1,), (1,)), ((), ())),
            preferred_element_type=F32,
        )

    acc[...] = add(msg_ref[me, 0:half, :], msg_ref[me, half : half + 16, :])

    @pl.loop(1, devices)
    def _(d):
        message(d).wait_recv()
        acc[...] += add(got[d, 0:half, :], got[d, half : half + 16, :])

    for h in range(8):
        inv = jnp.maximum(acc[512 + h : 513 + h, :], 1.0)
        mean = (acc[h * 64 : (h + 1) * 64, :] / inv).astype(BF16).astype(F32)
        bev[2 * h + 1] = mean[:, 0:128]
        bev[2 * h + 2] = mean[:, 128:256]

    lane = lax.broadcasted_iota(jnp.int32, (64, 128), 1)
    first = jnp.zeros((64, 128), F32)
    last = jnp.zeros((64, 128), F32)
    for r in range(TILE_Y):
        row = bev[r + 1]
        first = jnp.where(lane == r, row if r == 0 else pltpu.roll(row, r, 1), first)
        last = jnp.where(lane == r, pltpu.roll(row, r + 1, 1), last)
    edges[0] = first.astype(BF16)
    edges[1] = last.astype(BF16)
    edges[2] = bev[1].astype(BF16)
    edges[3] = bev[TILE_Y].astype(BF16)

    plans = []
    for dy in (-1, 0, 1):
        for dx in (-1, 0, 1):
            if dx == 0 and dy == 0:
                continue
            source = (0 if dx < 0 else 1) if dx else (2 if dy < 0 else 3)
            plans.append((dy, dx, source))
    copies = []
    for i, (dy, dx, source) in enumerate(plans):
        copy = pltpu.make_async_remote_copy(
            src_ref=edges.at[source],
            dst_ref=rims.at[i],
            send_sem=rim_send.at[i],
            recv_sem=rim_recv.at[i],
            device_id=(lax.rem(az + dy + az_count, az_count), lax.rem(el + dx + el_count, el_count)),
            device_id_type=mesh_id,
        )
        copy.start()
        copies.append(copy)

    @pl.loop(1, devices)
    def _(d):
        message(d).wait_send()

    for copy in copies:
        copy.wait()

    def rim(y, x):
        i = [(p[0], p[1]) for p in plans].index((-y, -x))
        there = jnp.logical_and(
            jnp.logical_and(az + y >= 0, az + y < az_count),
            jnp.logical_and(el + x >= 0, el + x < el_count),
        )
        return rims[i].astype(F32) * jnp.where(there, 1.0, 0.0)

    bev[0] = rim(-1, 0)
    bev[TILE_Y + 1] = rim(1, 0)
    for j, (y, x) in enumerate([(0, -1), (0, 1), (-1, -1), (-1, 1), (1, -1), (1, 1)]):
        ends[j] = rim(y, x)
    for r in range(TILE_Y + 2):
        row = bev[r]
        if r == 0:
            lhs, rhs, at = ends[2], ends[3], TILE_Y - 1
        elif r == TILE_Y + 1:
            lhs, rhs, at = ends[4], ends[5], 0
        else:
            lhs, rhs, at = ends[0], ends[1], r - 1
        before = lhs if at == 0 else pltpu.roll(lhs, 128 - at, 1)
        after = pltpu.roll(rhs, 127 - at, 1)
        views[r * 192 : r * 192 + 64, :] = jnp.where(
            lane == 0, before, pltpu.roll(row, 1, 1)
        ).astype(BF16)
        views[r * 192 + 64 : r * 192 + 128, :] = row.astype(BF16)
        views[r * 192 + 128 : r * 192 + 192, :] = jnp.where(
            lane == 127, after, pltpu.roll(row, 127, 1)
        ).astype(BF16)

    for s in range(TILE_Y // 2):
        r = 2 * s
        stack = jnp.concatenate(
            [views[r * 192 : r * 192 + 576, :], views[(r + 1) * 192 : (r + 1) * 192 + 576, :]],
            axis=1,
        )
        res = jnp.dot(head_ref[...], stack, preferred_element_type=F32)
        res = jnp.maximum(res + bias_ref[...], 0.0).astype(BF16)
        out_ref[r] = res[:, 0:128]
        out_ref[r + 1] = res[:, 128:256]


def block_pair(w):
    zero = jnp.zeros_like(w)
    return jnp.concatenate(
        [jnp.concatenate([w, zero], axis=-1), jnp.concatenate([zero, w], axis=-1)], axis=-2
    )


def on_device(
    features, points_xyz, return_mask, owner_tile, bev_cell,
    meta_proj, meta_bias, conv_weight, norm_gain, head_weight, head_bias,
):
    height, breadth = return_mask.shape
    az_count = lax.axis_size("az")
    el_count = lax.axis_size("el")
    devices = az_count * el_count
    count_pts = height * breadth
    cap = 2 * count_pts // devices

    flat = jnp.concatenate(
        [
            features, points_xyz, points_xyz, points_xyz, return_mask.astype(BF16)[None],
            jnp.zeros((54, height, breadth), BF16),
        ],
        axis=0,
    )
    main = flat.transpose(1, 2, 0)

    def swap(head, tail, axis, closed):
        count = lax.axis_size(axis)
        ends = count if closed else count - 1
        return (
            lax.ppermute(tail, axis, [(i, (i + 1) % count) for i in range(ends)]),
            lax.ppermute(head, axis, [((i + 1) % count, i) for i in range(ends)]),
        )

    left, right = swap(main[:, :2], main[:, breadth - 2 :], "az", True)
    top, low = swap(
        jnp.concatenate([left[:2], main[:2], right[:2]], axis=1),
        jnp.concatenate([left[height - 2 :], main[height - 2 :], right[height - 2 :]], axis=1),
        "el",
        False,
    )

    proj = meta_proj * 0.5
    top_w = lax.reduce_precision(proj, 8, 7)
    mid_w = lax.reduce_precision(proj - top_w, 8, 7)
    low_w = lax.reduce_precision(proj - top_w - mid_w, 8, 7)
    nil = jnp.zeros((CH, CH), F32)
    tail = jnp.zeros((54, CH), F32)
    flag = jnp.ones((1, CH), F32)
    wide = []
    for l in range(2):
        wide.append(jnp.concatenate([nil, top_w[l], mid_w[l], low_w[l], 0.0 * flag, tail], axis=0))
    wide.append(jnp.concatenate([nil, jnp.zeros((9, CH), F32), flag, tail], axis=0))
    wide.append(jnp.concatenate([jnp.eye(CH, dtype=F32), jnp.zeros((10, CH), F32), tail], axis=0))
    waux = jnp.concatenate([block_pair(w) for w in wide], axis=1).astype(BF16)
    bias = jnp.concatenate([meta_bias, meta_bias], axis=1) * 0.5
    gain = jnp.concatenate([norm_gain, norm_gain], axis=1)
    conv = block_pair(conv_weight).reshape(2, 9 * 128, 128)
    mean = block_pair(jnp.full((CH, CH), 1.0 / CH, BF16))

    owners = owner_tile.reshape(-1)
    cells = bev_cell.reshape(-1)
    keep = return_mask.reshape(-1)
    ranks = slot_ranks(owners, devices)
    target = owners * cap + ranks
    member = owners[None, :] == jnp.arange(devices, dtype=jnp.int32)[:, None]
    hi = jnp.where(keep > 0, cells // 256 + 1, 0)
    lo = jnp.where(keep > 0, cells % 256 + 1, 0)
    value = jnp.stack([hi, lo], axis=0).astype(BF16)
    tile_hot = jnp.where(member[None], value[:, None, :], 0).astype(BF16)
    rank_hot = (ranks[:, None] == jnp.arange(cap, dtype=jnp.int32)[None, :]).astype(BF16)
    labels = jnp.einsum("vtp,pr->tvr", tile_hot, rank_hot, preferred_element_type=F32) - 1.0
    lanes = min(cap, 128)
    labels = labels.reshape(devices, 2, cap // lanes, lanes)
    labels = jnp.pad(
        labels, ((0, 0), (0, 0), (0, 8 - cap // lanes), (0, 128 - lanes))
    ).reshape(devices, 16, 128).astype(BF16)

    vm = pl.BlockSpec(memory_space=pltpu.VMEM)
    deep = cap // 2 + 16
    plane = pltpu.VMEM((height + 4, WIDE, 128), F32)
    msg = pl.pallas_call(
        lambda *refs: layers_kernel(height, devices, cap, *refs),
        out_shape=jax.ShapeDtypeStruct((devices, deep, 128), BF16),
        in_specs=[pl.BlockSpec(memory_space=pltpu.SMEM)] + [vm] * 11,
        out_specs=vm,
        scratch_shapes=[
            plane, plane, plane, plane,
            pltpu.VMEM((height + 2, 136, 128), F32),
            pltpu.VMEM((512, 9 * 128), BF16),
            pltpu.VMEM((count_pts, 128), F32),
            pltpu.VMEM((devices * cap, 128), F32),
            pltpu.VMEM((2, 272, 128), F32),
        ],
        compiler_params=pltpu.CompilerParams(vmem_limit_bytes=56 << 20),
        name="layers",
    )(target, main, left, right, top, low, waux, bias, gain, conv, mean, labels)

    head = head_weight.reshape(9 * CH, HEAD_CH).T
    grid = pl.pallas_call(
        lambda *refs: cells_kernel(cap, az_count, el_count, *refs),
        out_shape=jax.ShapeDtypeStruct((TILE_Y, HEAD_CH, TILE_X), BF16),
        in_specs=[vm] * 3,
        out_specs=vm,
        scratch_shapes=[
            pltpu.VMEM((devices, deep, 128), BF16),
            pltpu.VMEM((528, 256), F32),
            pltpu.VMEM((TILE_Y + 2, CH, 128), F32),
            pltpu.VMEM((4, CH, 128), BF16),
            pltpu.VMEM((8, CH, 128), BF16),
            pltpu.VMEM((6, CH, 128), F32),
            pltpu.VMEM(((TILE_Y + 2) * 3 * CH, 128), BF16),
            pltpu.SemaphoreType.DMA((devices,)),
            pltpu.SemaphoreType.DMA((devices,)),
            pltpu.SemaphoreType.DMA((8,)),
            pltpu.SemaphoreType.DMA((8,)),
        ],
        compiler_params=pltpu.CompilerParams(
            vmem_limit_bytes=56 << 20, collective_id=0, has_side_effects=True
        ),
        name="cells",
    )(msg, head, head_bias[:, None])
    return grid.transpose(1, 0, 2)


def solution(mesh):
    placed = (
        P(None, "el", "az"),
        P(None, "el", "az"),
        P("el", "az"),
        P("el", "az"),
        P("el", "az"),
        P(),
        P(),
        P(),
        P(),
        P(),
        P(),
    )
    return jax.shard_map(
        on_device, mesh=mesh, in_specs=placed, out_specs=P(None, "az", "el"), check_vma=False
    )
```

time: 191 us -> 149 us (0.78)
  blocking collectives: 56.6 us -> 0 us
  Pallas kernels: 58.4 us -> 99.9 us
  other arithmetic: 15.9 us -> 4.29 us
  waiting for transfers between devices: 13.9 us -> 2.36 us
  local copies, waits for them, and re-layouts: 19.2 us -> 29.2 us
  starting transfers between devices: 16.7 us -> 8.95 us
  matrix products: 7.89 us -> 3.27 us
    all_to_all x1 -> x0, blocking collectives: 56.6 us -> none  [on_device(): lax.all_to_all(msg, ('az', 'el'), split_axis=0, concat_axis=0, tiled=True)]
    pallas_call x1, Pallas kernels: 21.1 us -> 64.5 us  [on_device(): pl.pallas_call(lambda *refs: cells_kernel(cap, az_count, el_count, *refs)...]
    ppermute x8 -> x4, waiting for transfers between devices: 13.9 us -> 2.36 us  [the longest x2 2.36 us: swap(): lax.ppermute(head, axis, [((i + 1) % count, i) for i in range(ends)])]
    concatenate x1 -> x4, local copies, waits for them, and re-layouts: 5.06 us -> 14 us  [the longest x1 13.3 us: on_device(): jnp.concatenate([features, points_xyz, points_xyz, points_xyz, return_mas...]
    ppermute x8 -> x4, starting transfers between devices: 16.7 us -> 8.95 us  [the longest x2 4.71 us: swap(): lax.ppermute(tail, axis, [(i, (i + 1) % count) for i in range(ends)])]
    transpose x1 -> x0, other arithmetic: 5.74 us -> none  [on_device(): turned = stacked.transpose(1, 2, 0)]
    dot_general x10 -> x1, matrix products: 7.41 us -> 2.79 us  [on_device(): jnp.einsum('vtp,pr->tvr', tile_hot, rank_hot, preferred_element_type=F32)]
    pad x2 -> x0, local copies, waits for them, and re-layouts: 3.42 us -> none  [the longest x1 2.81 us: on_device(): jnp.pad(jnp.concatenate([spots, spots, spots], axis=2), ((0, 0), (0, WIDE...]
  transfers between devices with their start and end apart: 8 -> 4, of which waited for: 5 -> 1; matrix products, arithmetic and copies ran while one was open for 5% -> 8% of each run, Pallas kernels for 0% -> 0%
where the time goes in v1:
time: 149 us; the launch traced here: 148 us
  Pallas kernels  99.9 us (67%)
  local copies, waits for them, and re-layouts  29.2 us (20%)
  starting transfers between devices  8.95 us (6%)
  other arithmetic  4.29 us (3%)
  matrix products  3.27 us (2%)
  waiting for transfers between devices  2.36 us (2%)
    pallas_call x1, Pallas kernels, on_device(): pl.pallas_call(lambda *refs: cells_kernel(cap, az_count, el_count, *refs)...  64.5 us
    pallas_call x1, Pallas kernels, on_device(): pl.pallas_call(lambda *refs: layers_kernel(height, devices, cap, *refs),...  35.5 us
    concatenate x1, local copies, waits for them, and re-layouts, on_device(): jnp.concatenate([features, points_xyz, points_xyz, points_xyz, return_mas...  13.3 us
    unnamed x35, local copies, waits for them, and re-layouts  5.05 us
    ppermute x2, starting transfers between devices, swap(): lax.ppermute(tail, axis, [(i, (i + 1) % count) for i in range(ends)])  4.71 us
    ppermute x2, starting transfers between devices, swap(): lax.ppermute(head, axis, [((i + 1) % count, i) for i in range(ends)])  4.24 us
  transfers between devices with their start and end apart: 4, of which 1 were waited for; matrix products, arithmetic and copies ran while one was open for 8% of the time, Pallas kernels for 0%

profile of v1, /device:TPU:0, one launch (start us, length us, event | category | flops | bytes accessed | tf_op | source)
XLA Modules:
  0.0 148.3 jit_solution(16894342680245471869)
XLA Ops:
  0.0 0.0 copy-start.4
  0.0 3.2 %copy.21 = bf16[64,32,256]{0,2,1:T(8,128)(2,1)} copy(bf16[64,32,256]{2,1,0:T(8,128)(2,1)} %param.11) | data formatting | bytes 2097152 | tf_op args[0]
  3.2 0.0 copy-done.7
  3.2 1.1 copy.22
  4.3 0.0 copy-done.4
  4.3 1.8 %copy.25 = bf16[1,32,256]{0,2,1:T(8,128)(2,1)} copy(bf16[1,32,256]{2,1,0:T(8,128)(2,1)S(1)} %convert_bitcast_fusion.1) | data formatting | bytes 32768 | tf_op jit(solution)/shard_map/broadcast_in_dim | solution.py:294
  6.1 1.9 %broadcast_in_dim.55 = bf16[54,32,256]{0,2,1:T(8,128)(2,1)} broadcast(bf16[]{:T(256)} %constant.27.clone.1), dimensions={} | broadcast | bytes 884738 | tf_op jit(solution)/shard_map/broadcast_in_dim | solution.py:295
  8.0 0.0 copy-start.5
  8.0 13.3 %concatenate.72 = bf16[128,32,256]{0,2,1:T(8,128)(2,1)} concatenate(bf16[64,32,256]{0,2,1:T(8,128)(2,1)} %copy.21, bf16[3,32,256]{0,2,1:T(8,128)(2,1)S(1)} %copy.22, bf16[3,32,256]{0,2,1:T(8,128)(2,1)S(1)} %copy.22, bf16[3,32,256]{0,2,1:T(8,128)(2,1)S(1)} %copy.22, bf16[1,32,256]{0,2,1:T(8,128)(2,1)} %copy.25, bf16[54,32,256]{0,2,1:T(8,128)(2,1)} %broadcast_in_dim.55), dimensions={0} | concatenate | bytes 4194304 | tf_op jit(solution)/shard_map/concatenate | solution.py:292
  21.3 0.0 copy-start.11
  21.3 0.0 copy-start.8
  21.3 0.9 fusion.62
  22.2 0.5 collective-permute-start
  22.8 2.9 %collective-permute-start.1 = (bf16[32,2,128]{2,1,0:T(2,128)(2,1)S(1)}, bf16[32,2,128]{2,1,0:T(2,128)(2,1)S(1)}, u32[]{:S(2)}, u32[]{:S(2)}) collective-permute-start(bf16[32,2,128]{2,1,0:T(2,128)(2,1)S(1)} %get-tuple-element.7), channel_id=1, source_target_pairs={{4,0},{8,4},{12,8},{16,12},{20,16},{24,20},{28,24},{0,28},{5,1},{9... | collective-permute-start | bytes 49160 | tf_op jit(solution)/shard_map/ppermute | solution.py:306
  25.7 1.0 fusion.61
  26.7 0.0 copy-done.5
  26.8 0.3 convert_reduce_fusion
  27.1 0.1 reduce_window_sum.11
  27.2 0.5 fusion.6
  27.7 0.6 multiply_add_fusion.refs_0_
  28.3 0.1 iota_compare_fusion.3
  28.5 0.0 copy-done.11
  28.6 0.0 copy-done.8
  28.6 0.3 select_convert_fusion
  28.9 0.1 pad_maximum_fusion.2
  29.0 0.0 copy-start.6
  29.0 0.0 copy-start.12
  29.1 0.0 copy-start.13
  29.1 0.0 copy-start.1
  29.1 0.0 copy-start.14
  29.1 2.8 %fusion.15 = bf16[32,2,512]{2,0,1:T(8,128)(2,1)S(1)} fusion(s32[8192]{0:T(1024)S(1)} %convert_bitcast_fusion, pred[32,8192]{1,0:T(8,128)(4,1)S(1)} %iota_compare_fusion.3, bf16[2,8192]{1,0:T(2,128)(2,1)S(1)} %pad_maximum_fusion.2), kind=kOutput, calls=%fused_computation.14 | convolution fusion | flops 541655040 | bytes 393216 | tf_op jit(solution)/shard_map/vtp,pr->tvr/dot_general | solution.py:346
  31.9 0.0 copy-start
  31.9 0.7 pad_bitcast_fusion.refs_11_
  32.6 0.1 pad.36.clone
  32.7 0.1 maximum_convert_fusion
  32.8 0.3 concatenate.79
  33.1 0.3 concatenate.75
  33.5 0.0 copy-done.6
  33.5 0.8 fusion.48.refs_6_
  34.3 0.0 collective-permute-done.1.refs_3_
  34.3 0.0 copy-start.10
  34.3 0.0 collective-permute-done.refs_2_
  34.3 0.0 copy-start.9
  34.4 4.2 %collective-permute-start.2 = (bf16[2,260,128]{2,1,0:T(8,128)(2,1)S(1)}, bf16[2,260,128]{2,1,0:T(8,128)(2,1)S(1)}, u32[]{:S(2)}, u32[]{:S(2)}) collective-permute-start(bf16[2,260,128]{2,1,0:T(8,128)(2,1)S(1)} %pad_maximum_fusion), channel_id=1, source_target_pairs={{0,1},{1,2},{2,3},{4,5},{5,6},{6,7},{8,9},{9,10},{10,11},{12,13},{... | collective-permute-start | bytes 399368 | tf_op jit(solution)/shard_map/ppermute | solution.py:305
  38.6 1.3 collective-permute-start.3
  39.9 0.0 copy-done.12
  39.9 0.0 copy-done.13
  39.9 0.7 maximum_multiply_fusion
  40.6 0.0 copy-done.1
  40.6 0.8 copy.28
  41.4 0.0 copy-done.14
  41.4 0.7 copy.29.refs_2_
  42.2 0.0 copy-done
  42.2 1.0 fusion.25
  43.2 0.0 collective-permute-done.2.refs_4_
  43.2 0.0 copy-start.2
  43.2 2.4 %collective-permute-done.3.refs_5_ = bf16[2,260,128]{2,1,0:T(8,128)(2,1)S(1)} collective-permute-done((bf16[2,260,128]{2,1,0:T(8,128)(2,1)S(1)}, bf16[2,260,128]{2,1,0:T(8,128)(2,1)S(1)}, u32[]{:S(2)}, u32[]{:S(2)}) %collective-permute-start.3) | collective-permute-done | bytes 133152 | tf_op jit(solution)/shard_map/ppermute | solution.py:306
  45.5 0.0 copy-done.10
  45.5 0.0 copy-done.9
  45.5 0.0 copy-done.2
  45.5 0.7 copy-done.3
  46.2 35.5 %layers.1.refs_0_ = bf16[32,272,128]{2,1,0:T(8,128)(2,1)} custom-call(s32[8192]{0:T(1024)} %multiply_add_fusion.refs_0_, bf16[32,256,128]{2,1,0:T(8,128)(2,1)} %bitcast.59, bf16[32,2,128]{2,1,0:T(2,128)(2,1)} %copy-done.9, bf16[32,2,128]{2,1,0:T(2,128)(2,1)} %copy-done.10, bf16[2,260,128]{2,1,0:T(8,128)(2,1)} %copy-done.2, bf16[2,260,128]{2,1,0:T(8,128)(2,1)} %copy-done.3, ...), custom_call_target="tpu_custom_call" | custom-call | tf_op jit(solution)/shard_map/layers/pallas_call | solution.py:356
  81.7 64.5 %cells.1 = bf16[16,128,128]{2,1,0:T(8,128)(2,1)} custom-call(bf16[32,272,128]{2,1,0:T(8,128)(2,1)} %layers.1.refs_0_, bf16[128,576]{1,0:T(8,128)(2,1)} %bitcast.62, f32[128,1]{1,0:T(8,128)} %copy.29.refs_2_), custom_call_target="tpu_custom_call" | custom-call | tf_op jit(solution)/shard_map/cells/pallas_call | solution.py:374
  146.2 2.2 %copy.30 = bf16[128,16,128]{2,1,0:T(8,128)(2,1)} copy(bf16[128,16,128]{2,0,1:T(8,128)(2,1)} %bitcast.61) | data formatting | bytes 1048576 | tf_op jit(solution)/shard_map/transpose | solution.py:397
  (23 shorter events, 0.3 us)
Async XLA Ops:
  0.0 3.2 %copy-start.7 = (bf16[3,32,256]{2,1,0:T(8,128)(2,1)S(1)}, bf16[3,32,256]{2,1,0:T(8,128)(2,1)}, u32[]{:S(2)}) copy-start(bf16[3,32,256]{2,1,0:T(8,128)(2,1)} %param.12) | copy-start | bytes 147460
  0.0 4.3 %copy-start.4 = (s32[32,256]{1,0:T(8,128)S(1)}, s32[32,256]{1,0:T(8,128)}, u32[]{:S(2)}) copy-start(s32[32,256]{1,0:T(8,128)} %param.13) | copy-start | bytes 98308
  8.0 18.7 %copy-start.5 = (s32[32,256]{1,0:T(8,128)S(1)}, s32[32,256]{1,0:T(8,128)}, u32[]{:S(2)}) copy-start(s32[32,256]{1,0:T(8,128)} %param.14) | copy-start | bytes 98308
  21.3 7.2 %copy-start.11 = (f32[2,3,64]{2,0,1:T(2,128)S(1)}, f32[2,3,64]{2,0,1:T(2,128)}, u32[]{:S(2)}) copy-start(f32[2,3,64]{2,0,1:T(2,128)} %param.16) | copy-start | bytes 4612
  21.3 7.3 %copy-start.8 = (s32[32,256]{1,0:T(8,128)S(1)}, s32[32,256]{1,0:T(8,128)}, u32[]{:S(2)}) copy-start(s32[32,256]{1,0:T(8,128)} %param.15) | copy-start | bytes 98308
  22.2 12.1 %collective-permute-start = (bf16[32,2,128]{2,1,0:T(2,128)(2,1)S(1)}, bf16[32,2,128]{2,1,0:T(2,128)(2,1)S(1)}, u32[]{:S(2)}, u32[]{:S(2)}) collective-permute-start(bf16[32,2,128]{2,1,0:T(2,128)(2,1)S(1)} %get-tuple-element.8), channel_id=1, source_target_pairs={{0,4},{4,8},{8,12},{12,16},{16,20},{20,24},{24,28},{28,0},{1,5},{5... | collective-permute-start | bytes 49160 | tf_op jit(solution)/shard_map/ppermute | solution.py:305
  22.8 11.5 %collective-permute-start.1 = (bf16[32,2,128]{2,1,0:T(2,128)(2,1)S(1)}, bf16[32,2,128]{2,1,0:T(2,128)(2,1)S(1)}, u32[]{:S(2)}, u32[]{:S(2)}) collective-permute-start(bf16[32,2,128]{2,1,0:T(2,128)(2,1)S(1)} %get-tuple-element.7), channel_id=1, source_target_pairs={{4,0},{8,4},{12,8},{16,12},{20,16},{24,20},{28,24},{0,28},{5,1},{9... | collective-permute-start | bytes 49160 | tf_op jit(solution)/shard_map/ppermute | solution.py:306
  29.0 4.5 %copy-start.6 = (bf16[256,128]{1,0:T(8,128)(2,1)S(1)}, bf16[256,128]{1,0:T(8,128)(2,1)}, u32[]{:S(2)}) copy-start(bf16[256,128]{1,0:T(8,128)(2,1)} %constant.52.clone.1) | copy-start | bytes 196612
  29.0 10.9 %copy-start.12 = (f32[2,64]{1,0:T(2,128)S(1)}, f32[2,64]{1,0:T(2,128)}, u32[]{:S(2)}) copy-start(f32[2,64]{1,0:T(2,128)} %param.17) | copy-start | bytes 1540
  29.1 10.9 %copy-start.13 = (f32[2,64]{1,0:T(2,128)S(1)}, f32[2,64]{1,0:T(2,128)}, u32[]{:S(2)}) copy-start(f32[2,64]{1,0:T(2,128)} %param.19) | copy-start | bytes 1540
  29.1 11.6 %copy-start.1 = (bf16[9,64,128]{2,1,0:T(8,128)(2,1)S(1)}, bf16[9,64,128]{2,1,0:T(8,128)(2,1)}, u32[]{:S(2)}) copy-start(bf16[9,64,128]{2,1,0:T(8,128)(2,1)} %param.20) | copy-start | bytes 442372
  29.1 12.3 %copy-start.14 = (f32[128]{0:T(128)S(1)}, f32[128]{0:T(128)}, u32[]{:S(2)}) copy-start(f32[128]{0:T(128)} %param.21) | copy-start | bytes 1540
  31.9 10.3 %copy-start = (bf16[2,9,64,64]{3,2,1,0:T(8,128)(2,1)S(1)}, bf16[2,9,64,64]{3,2,1,0:T(8,128)(2,1)}, u32[]{:S(2)}) copy-start(bf16[2,9,64,64]{3,2,1,0:T(8,128)(2,1)} %param.18) | copy-start | bytes 442372
  34.3 11.2 %copy-start.10 = (bf16[32,2,128]{2,1,0:T(2,128)(2,1)}, bf16[32,2,128]{2,1,0:T(2,128)(2,1)S(1)}, u32[]{:S(2)}) copy-start(bf16[32,2,128]{2,1,0:T(2,128)(2,1)S(1)} %collective-permute-done.1.refs_3_) | copy-start | bytes 49156
  34.3 11.2 %copy-start.9 = (bf16[32,2,128]{2,1,0:T(2,128)(2,1)}, bf16[32,2,128]{2,1,0:T(2,128)(2,1)S(1)}, u32[]{:S(2)}) copy-start(bf16[32,2,128]{2,1,0:T(2,128)(2,1)S(1)} %collective-permute-done.refs_2_) | copy-start | bytes 49156
  34.4 8.8 %collective-permute-start.2 = (bf16[2,260,128]{2,1,0:T(8,128)(2,1)S(1)}, bf16[2,260,128]{2,1,0:T(8,128)(2,1)S(1)}, u32[]{:S(2)}, u32[]{:S(2)}) collective-permute-start(bf16[2,260,128]{2,1,0:T(8,128)(2,1)S(1)} %pad_maximum_fusion), channel_id=1, source_target_pairs={{0,1},{1,2},{2,3},{4,5},{5,6},{6,7},{8,9},{9,10},{10,11},{12,13},{... | collective-permute-start | bytes 399368 | tf_op jit(solution)/shard_map/ppermute | solution.py:305
  38.6 6.9 %collective-permute-start.3 = (bf16[2,260,128]{2,1,0:T(8,128)(2,1)S(1)}, bf16[2,260,128]{2,1,0:T(8,128)(2,1)S(1)}, u32[]{:S(2)}, u32[]{:S(2)}) collective-permute-start(bf16[2,260,128]{2,1,0:T(8,128)(2,1)S(1)} %pad_maximum_fusion.1), channel_id=1, source_target_pairs={{1,0},{2,1},{3,2},{5,4},{6,5},{7,6},{9,8},{10,9},{11,10},{13,12},{... | collective-permute-start | bytes 399368 | tf_op jit(solution)/shard_map/ppermute | solution.py:306
  43.2 2.4 %copy-start.2 = (bf16[2,260,128]{2,1,0:T(8,128)(2,1)}, bf16[2,260,128]{2,1,0:T(8,128)(2,1)S(1)}, u32[]{:S(2)}) copy-start(bf16[2,260,128]{2,1,0:T(8,128)(2,1)S(1)} %collective-permute-done.2.refs_4_) | copy-start | bytes 399364
  45.5 0.7 copy-start.3

commit v2 on v1

--- a/solution.py
+++ b/solution.py
@@ -30,6 +30,20 @@
     return ranks.reshape(-1).astype(jnp.int32)
 
 
+def turn_kernel(feat_ref, spot_ref, mask_ref, out_ref):
+    rest = jnp.zeros((54, feat_ref.shape[2]), F32)
+
+    @pl.loop(0, feat_ref.shape[0] // 2)
+    def _(s):
+        for u in range(2):
+            r = s * 2 + u
+            spot = spot_ref[r].astype(F32)
+            flag = mask_ref[pl.ds(r, 1), :].astype(F32)
+            tail = jnp.concatenate([spot, spot, spot, flag, rest], axis=0).astype(BF16)
+            both = jnp.concatenate([feat_ref[r], tail], axis=0)
+            out_ref[r] = jnp.transpose(both)
+
+
 def layers_kernel(
     height, tiles, cap,
     tgt_ref, main_ref, left_ref, right_ref, top_ref, low_ref,
@@ -66,9 +80,11 @@
             line[u, 258:260, :] = right_ref[r].astype(F32)
             place(u, r + 2)
 
-    def layer(l, rows, width, per, q, x, qrow, qcol, emit):
+    def layer(l, rows, width, per, q, x, qrow, qcol, emit, beside=None):
         @pl.loop(0, rows // per)
         def _(s):
+            if beside is not None:
+                beside(s)
             for u in range(per):
                 r = s * per + u
                 shift = q[r + 1 + qrow, pl.ds(1 + qcol, width), :] - bias_ref[l : l + 1, :]
@@ -96,15 +112,18 @@
         pts[pl.ds(pl.multiple_of(r * 256 + 128, 128), 128), :] = pltpu.roll(new, 64, 1)
 
     layer(0, height + 2, 136, 2, q1, x0, 0, 0, emit1)
-    layer(1, height, 128, 4, q2, x1, 1, 1, emit2)
-
-    unroll = 64
-
-    @pl.loop(0, height * 256 // unroll)
+    def scatter(base, count):
+        for u in range(count):
+            dest[pl.ds(tgt_ref[base + u], 1), :] = pts[pl.ds(base + u, 1), :]
+
+    layer(
+        1, height, 128, 4, q2, x1, 1, 1, emit2,
+        lambda s: scatter(pl.multiple_of(jnp.maximum(s - 1, 0) * 1024, 1024), 1024),
+    )
+
+    @pl.loop(0, 16)
     def _(i):
-        base = i * unroll
-        for u in range(unroll):
-            dest[pl.ds(tgt_ref[base + u], 1), :] = pts[pl.ds(base + u, 1), :]
+        scatter((height - 4) * 256 + pl.multiple_of(i * 64, 64), 64)
 
     left = lax.broadcasted_iota(jnp.int32, (cap // 2, 128), 1) < 64
 
@@ -120,8 +139,8 @@
     cap, az_count, el_count,
     msg_ref, head_ref, bias_ref,
     out_ref,
-    got, acc, bev, edges, rims, ends, views,
-    send_sem, recv_sem, rim_send, rim_recv,
+    got, acc, part, part_in, tally, tally_in, bev, edges, rims, ends, views,
+    part_send, part_recv, send_sem, recv_sem, rim_send, rim_recv,
 ):
     az, el = lax.axis_index("az"), lax.axis_index("el")
     devices = az_count * el_count
@@ -140,20 +159,25 @@
 
     pl.semaphore_wait(barrier, devices - 1)
 
-    def message(d):
-        other, where = spot(d)
+    others = az_count - 1
+
+    def message(k, d):
+        column = lax.rem(el + k + 1, el_count)
+        row = lax.rem(az + d, az_count)
         return pltpu.make_async_remote_copy(
-            src_ref=msg_ref.at[other],
-            dst_ref=got.at[d],
-            send_sem=send_sem.at[d],
-            recv_sem=recv_sem.at[d],
-            device_id=where,
+            src_ref=msg_ref.at[row * el_count + column],
+            dst_ref=got.at[k * others + d - 1],
+            send_sem=send_sem.at[k * others + d - 1],
+            recv_sem=recv_sem.at[k * others + d - 1],
+            device_id=(row, el),
             device_id_type=mesh_id,
         )
 
-    @pl.loop(1, devices)
-    def _(d):
-        message(d).start()
+    for k in range(el_count):
+
+        @pl.loop(1, az_count)
+        def _(d):
+            message(k, d).start()
 
     half = cap // 2
     lanes = min(cap, 128)
@@ -177,12 +201,38 @@
             preferred_element_type=F32,
         )
 
-    acc[...] = add(msg_ref[me, 0:half, :], msg_ref[me, half : half + 16, :])
-
-    @pl.loop(1, devices)
-    def _(d):
-        message(d).wait_recv()
-        acc[...] += add(got[d, 0:half, :], got[d, half : half + 16, :])
+    partials = []
+    for k in range(el_count):
+        column = lax.rem(el + k + 1, el_count)
+        own = az * el_count + column
+        acc[...] = add(msg_ref[own, 0:half, :], msg_ref[own, half : half + 16, :])
+
+        @pl.loop(1, az_count)
+        def _(d):
+            message(k, d).wait_recv()
+            slot = k * others + d - 1
+            acc[...] += add(got[slot, 0:half, :], got[slot, half : half + 16, :])
+
+        if k < el_count - 1:
+            part[k] = acc[0:512, :].astype(BF16)
+            tally[k] = acc[512:528, :]
+            for i, (src, dst) in enumerate(((part, part_in), (tally, tally_in))):
+                copy = pltpu.make_async_remote_copy(
+                    src_ref=src.at[k],
+                    dst_ref=dst.at[k],
+                    send_sem=part_send.at[2 * k + i],
+                    recv_sem=part_recv.at[2 * k + i],
+                    device_id=(az, column),
+                    device_id_type=mesh_id,
+                )
+                copy.start()
+                partials.append(copy)
+
+    for k in range(el_count - 1):
+        partials[2 * k].wait_recv()
+        partials[2 * k + 1].wait_recv()
+        acc[0:512, :] += part_in[k].astype(F32)
+        acc[512:528, :] += tally_in[k]
 
     for h in range(8):
         inv = jnp.maximum(acc[512 + h : 513 + h, :], 1.0)
@@ -222,9 +272,14 @@
         copy.start()
         copies.append(copy)
 
-    @pl.loop(1, devices)
-    def _(d):
-        message(d).wait_send()
+    for k in range(el_count):
+
+        @pl.loop(1, az_count)
+        def _(d):
+            message(k, d).wait_send()
+
+    for copy in partials:
+        copy.wait_send()
 
     for copy in copies:
         copy.wait()
@@ -289,14 +344,14 @@
     count_pts = height * breadth
     cap = 2 * count_pts // devices
 
-    flat = jnp.concatenate(
-        [
-            features, points_xyz, points_xyz, points_xyz, return_mask.astype(BF16)[None],
-            jnp.zeros((54, height, breadth), BF16),
-        ],
-        axis=0,
-    )
-    main = flat.transpose(1, 2, 0)
+    main = pl.pallas_call(
+        turn_kernel,
+        out_shape=jax.ShapeDtypeStruct((height, breadth, 128), BF16),
+        in_specs=[pl.BlockSpec(memory_space=pltpu.VMEM)] * 3,
+        out_specs=pl.BlockSpec(memory_space=pltpu.VMEM),
+        compiler_params=pltpu.CompilerParams(vmem_limit_bytes=56 << 20),
+        name="turn",
+    )(features.transpose(1, 0, 2), points_xyz.transpose(1, 0, 2), return_mask)
 
     def swap(head, tail, axis, closed):
         count = lax.axis_size(axis)
@@ -377,15 +432,21 @@
         in_specs=[vm] * 3,
         out_specs=vm,
         scratch_shapes=[
-            pltpu.VMEM((devices, deep, 128), BF16),
+            pltpu.VMEM((devices - el_count, deep, 128), BF16),
             pltpu.VMEM((528, 256), F32),
+            pltpu.VMEM((el_count - 1, 512, 256), BF16),
+            pltpu.VMEM((el_count - 1, 512, 256), BF16),
+            pltpu.VMEM((el_count - 1, 16, 256), F32),
+            pltpu.VMEM((el_count - 1, 16, 256), F32),
             pltpu.VMEM((TILE_Y + 2, CH, 128), F32),
             pltpu.VMEM((4, CH, 128), BF16),
             pltpu.VMEM((8, CH, 128), BF16),
             pltpu.VMEM((6, CH, 128), F32),
             pltpu.VMEM(((TILE_Y + 2) * 3 * CH, 128), BF16),
-            pltpu.SemaphoreType.DMA((devices,)),
-            pltpu.SemaphoreType.DMA((devices,)),
+            pltpu.SemaphoreType.DMA((2 * el_count - 2,)),
+            pltpu.SemaphoreType.DMA((2 * el_count - 2,)),
+            pltpu.SemaphoreType.DMA((devices - el_count,)),
+            pltpu.SemaphoreType.DMA((devices - el_count,)),
             pltpu.SemaphoreType.DMA((8,)),
             pltpu.SemaphoreType.DMA((8,)),
         ],

time: 149 us -> 118 us (0.79)
  local copies, waits for them, and re-layouts: 29.2 us -> 11.4 us
  Pallas kernels: 99.9 us -> 89 us
  waiting for transfers between devices: 2.36 us -> 0.01 us
    pallas_call x1, Pallas kernels: 64.5 us -> 49.4 us  [on_device(): pl.pallas_call(lambda *refs: cells_kernel(cap, az_count, el_count, *refs)...]
    concatenate x1 -> x0, local copies, waits for them, and re-layouts: 13.3 us -> none  [on_device(): jnp.concatenate([features, points_xyz, points_xyz, points_xyz, return_mas...]
    pallas_call x0 -> x1, Pallas kernels: none -> 3.98 us  [on_device(): pl.pallas_call(turn_kernel, out_shape=jax.ShapeDtypeStruct((height, bread...]
    broadcast_in_dim x2 -> x0, local copies, waits for them, and re-layouts: 3.71 us -> none  [the longest x1 1.87 us: on_device(): jnp.zeros((54, height, breadth), BF16)]
    ppermute x2, waiting for transfers between devices: 2.36 us -> 0.01 us  [swap(): lax.ppermute(head, axis, [((i + 1) % count, i) for i in range(ends)])]
  transfers between devices with their start and end apart: 4 -> 4, of which waited for: 1 -> 0; matrix products, arithmetic and copies ran while one was open for 8% -> 10% of each run, Pallas kernels for 0% -> 0%
where the time goes in v2:
time: 118 us
  Pallas kernels  89 us (75%)
  local copies, waits for them, and re-layouts  11.4 us (10%)
  starting transfers between devices  9.73 us (8%)
  other arithmetic  4.28 us (4%)
  matrix products  3.27 us (3%)
    pallas_call x1, Pallas kernels, on_device(): pl.pallas_call(lambda *refs: cells_kernel(cap, az_count, el_count, *refs)...  49.4 us
    pallas_call x1, Pallas kernels, on_device(): pl.pallas_call(lambda *refs: layers_kernel(height, devices, cap, *refs),...  35.6 us
    ppermute x2, starting transfers between devices, swap(): lax.ppermute(tail, axis, [(i, (i + 1) % count) for i in range(ends)])  5.49 us
    unnamed x35, local copies, waits for them, and re-layouts  4.3 us
    ppermute x2, starting transfers between devices, swap(): lax.ppermute(head, axis, [((i + 1) % count, i) for i in range(ends)])  4.24 us
    pallas_call x1, Pallas kernels, on_device(): pl.pallas_call(turn_kernel, out_shape=jax.ShapeDtypeStruct((height, bread...  3.98 us
    dot_general x1, matrix products, on_device(): jnp.einsum('vtp,pr->tvr', tile_hot, rank_hot, preferred_element_type=F32)  2.79 us
  transfers between devices with their start and end apart: 4, of which 0 were waited for; matrix products, arithmetic and copies ran while one was open for 10% of the time, Pallas kernels for 0%

profile of v2, /device:TPU:0, one launch (start us, length us, event | category | flops | bytes accessed | tf_op | source)
XLA Modules:
  0.0 118.0 jit_solution(14160870624108051919)
XLA Ops:
  0.0 0.0 copy-start.7
  0.0 2.8 %copy.46 = bf16[64,32,256]{2,0,1:T(8,128)(2,1)} copy(bf16[64,32,256]{2,1,0:T(8,128)(2,1)} %param.11) | data formatting | bytes 2097152 | tf_op args[0]
  2.8 0.0 copy-done.7
  2.8 0.0 copy-start.4
  2.8 0.0 copy-start.5
  2.8 0.7 copy.47
  3.5 4.0 %turn.1.refs_1_ = bf16[32,256,128]{2,1,0:T(8,128)(2,1)} custom-call(bf16[32,64,256]{2,1,0:T(8,128)(2,1)} %bitcast.60, bf16[32,3,256]{2,1,0:T(4,128)(2,1)} %bitcast.66, s32[32,256]{1,0:T(8,128)} %mask_ref.1), custom_call_target="tpu_custom_call" | custom-call | tf_op jit(solution)/shard_map/turn/pallas_call | solution.py:347
  7.5 0.0 copy-start.11
  7.5 0.0 copy-start.8
  7.5 0.9 fusion.62
  8.4 0.5 collective-permute-start
  8.9 2.9 %collective-permute-start.1 = (bf16[32,2,128]{2,1,0:T(2,128)(2,1)S(1)}, bf16[32,2,128]{2,1,0:T(2,128)(2,1)S(1)}, u32[]{:S(2)}, u32[]{:S(2)}) collective-permute-start(bf16[32,2,128]{2,1,0:T(2,128)(2,1)S(1)} %get-tuple-element.7), channel_id=1, source_target_pairs={{4,0},{8,4},{12,8},{16,12},{20,16},{24,20},{28,24},{0,28},{5,1},{9... | collective-permute-start | bytes 49160 | tf_op jit(solution)/shard_map/ppermute | solution.py:361
  11.8 1.0 fusion.61
  12.8 0.0 copy-done.4
  12.9 0.0 copy-done.5
  12.9 0.3 convert_reduce_fusion
  13.2 0.1 reduce_window_sum.11
  13.3 0.5 fusion.6
  13.9 0.1 iota_compare_fusion.3
  14.0 0.6 multiply_add_fusion.refs_0_
  14.6 0.0 copy-done.11
  14.7 0.0 copy-done.8
  14.7 0.3 select_convert_fusion
  15.1 0.1 pad_maximum_fusion.2
  15.2 0.0 copy-start.6
  15.2 0.0 copy-start.12
  15.2 0.0 copy-start.13
  15.2 0.0 copy-start.1
  15.2 0.0 copy-start.14
  15.2 2.8 %fusion.15 = bf16[32,2,512]{2,0,1:T(8,128)(2,1)S(1)} fusion(s32[8192]{0:T(1024)S(1)} %convert_bitcast_fusion, pred[32,8192]{1,0:T(8,128)(4,1)S(1)} %iota_compare_fusion.3, bf16[2,8192]{1,0:T(2,128)(2,1)S(1)} %pad_maximum_fusion.2), kind=kOutput, calls=%fused_computation.14 | convolution fusion | flops 541655040 | bytes 393216 | tf_op jit(solution)/shard_map/vtp,pr->tvr/dot_general | solution.py:401
  18.0 0.0 copy-start
  18.0 0.7 pad_bitcast_fusion.refs_11_
  18.7 0.1 pad.36.clone
  18.8 0.1 maximum_convert_fusion
  18.9 0.3 concatenate.71
  19.3 0.3 concatenate.75
  19.6 0.0 copy-done.6
  19.6 0.8 fusion.48.refs_6_
  20.4 0.0 collective-permute-done.refs_2_
  20.4 0.0 copy-start.9
  20.4 0.0 collective-permute-done.1.refs_3_
  20.4 0.0 copy-start.10
  20.5 1.3 %collective-permute-start.3 = (bf16[2,260,128]{2,1,0:T(8,128)(2,1)S(1)}, bf16[2,260,128]{2,1,0:T(8,128)(2,1)S(1)}, u32[]{:S(2)}, u32[]{:S(2)}) collective-permute-start(bf16[2,260,128]{2,1,0:T(8,128)(2,1)S(1)} %pad_maximum_fusion.1), channel_id=1, source_target_pairs={{1,0},{2,1},{3,2},{5,4},{6,5},{7,6},{9,8},{10,9},{11,10},{13,12},{... | collective-permute-start | bytes 399368 | tf_op jit(solution)/shard_map/ppermute | solution.py:361
  21.9 5.0 %collective-permute-start.2 = (bf16[2,260,128]{2,1,0:T(8,128)(2,1)S(1)}, bf16[2,260,128]{2,1,0:T(8,128)(2,1)S(1)}, u32[]{:S(2)}, u32[]{:S(2)}) collective-permute-start(bf16[2,260,128]{2,1,0:T(8,128)(2,1)S(1)} %pad_maximum_fusion), channel_id=1, source_target_pairs={{0,1},{1,2},{2,3},{4,5},{5,6},{6,7},{8,9},{9,10},{10,11},{12,13},{... | collective-permute-start | bytes 399368 | tf_op jit(solution)/shard_map/ppermute | solution.py:360
  26.9 0.0 copy-done.12
  26.9 0.0 copy-done.13
  26.9 0.7 maximum_multiply_fusion
  27.5 0.0 copy-done.1
  27.5 0.8 copy.23
  28.3 0.0 copy-done.14
  28.3 0.7 copy.24.refs_2_
  29.1 0.0 copy-done
  29.1 1.0 fusion.25
  30.1 0.0 collective-permute-done.3.refs_5_
  30.1 0.0 copy-start.2
  30.1 0.0 collective-permute-done.2.refs_4_
  30.1 0.0 copy-start.3
  30.1 0.0 copy-done.9
  30.1 0.0 copy-done.10
  30.1 0.6 copy-done.2
  30.8 0.0 copy-done.3
  30.8 35.6 %layers.1.refs_0_ = bf16[32,272,128]{2,1,0:T(8,128)(2,1)} custom-call(s32[8192]{0:T(1024)} %multiply_add_fusion.refs_0_, bf16[32,256,128]{2,1,0:T(8,128)(2,1)} %turn.1.refs_1_, bf16[32,2,128]{2,1,0:T(2,128)(2,1)} %copy-done.9, bf16[32,2,128]{2,1,0:T(2,128)(2,1)} %copy-done.10, bf16[2,260,128]{2,1,0:T(8,128)(2,1)} %copy-done.3, ...), custom_call_target="tpu_custom_call" | custom-call | tf_op jit(solution)/shard_map/layers/pallas_call | solution.py:411
  66.4 49.4 %cells.1 = bf16[16,128,128]{2,1,0:T(8,128)(2,1)} custom-call(bf16[32,272,128]{2,1,0:T(8,128)(2,1)} %layers.1.refs_0_, bf16[128,576]{1,0:T(8,128)(2,1)} %bitcast.63, f32[128,1]{1,0:T(8,128)} %copy.24.refs_2_), custom_call_target="tpu_custom_call" | custom-call | tf_op jit(solution)/shard_map/cells/pallas_call | solution.py:429
  115.9 2.2 %copy.25 = bf16[128,16,128]{2,1,0:T(8,128)(2,1)} copy(bf16[128,16,128]{2,0,1:T(8,128)(2,1)} %bitcast.62) | data formatting | bytes 1048576 | tf_op jit(solution)/shard_map/transpose | solution.py:458
  (20 shorter events, 0.3 us)
Async XLA Ops:
  0.0 2.8 %copy-start.7 = (bf16[3,32,256]{2,1,0:T(8,128)(2,1)S(1)}, bf16[3,32,256]{2,1,0:T(8,128)(2,1)}, u32[]{:S(2)}) copy-start(bf16[3,32,256]{2,1,0:T(8,128)(2,1)} %param.12) | copy-start | bytes 147460
  2.8 10.0 %copy-start.4 = (s32[32,256]{1,0:T(8,128)S(1)}, s32[32,256]{1,0:T(8,128)}, u32[]{:S(2)}) copy-start(s32[32,256]{1,0:T(8,128)} %mask_ref.1) | copy-start | bytes 98308
  2.8 10.1 %copy-start.5 = (s32[32,256]{1,0:T(8,128)S(1)}, s32[32,256]{1,0:T(8,128)}, u32[]{:S(2)}) copy-start(s32[32,256]{1,0:T(8,128)} %param.14) | copy-start | bytes 98308
  7.5 7.2 %copy-start.11 = (f32[2,3,64]{2,0,1:T(2,128)S(1)}, f32[2,3,64]{2,0,1:T(2,128)}, u32[]{:S(2)}) copy-start(f32[2,3,64]{2,0,1:T(2,128)} %param.16) | copy-start | bytes 4612
  7.5 7.2 %copy-start.8 = (s32[32,256]{1,0:T(8,128)S(1)}, s32[32,256]{1,0:T(8,128)}, u32[]{:S(2)}) copy-start(s32[32,256]{1,0:T(8,128)} %param.15) | copy-start | bytes 98308
  8.4 12.0 %collective-permute-start = (bf16[32,2,128]{2,1,0:T(2,128)(2,1)S(1)}, bf16[32,2,128]{2,1,0:T(2,128)(2,1)S(1)}, u32[]{:S(2)}, u32[]{:S(2)}) collective-permute-start(bf16[32,2,128]{2,1,0:T(2,128)(2,1)S(1)} %get-tuple-element.8), channel_id=1, source_target_pairs={{0,4},{4,8},{8,12},{12,16},{16,20},{20,24},{24,28},{28,0},{1,5},{5... | collective-permute-start | bytes 49160 | tf_op jit(solution)/shard_map/ppermute | solution.py:360
  8.9 11.5 %collective-permute-start.1 = (bf16[32,2,128]{2,1,0:T(2,128)(2,1)S(1)}, bf16[32,2,128]{2,1,0:T(2,128)(2,1)S(1)}, u32[]{:S(2)}, u32[]{:S(2)}) collective-permute-start(bf16[32,2,128]{2,1,0:T(2,128)(2,1)S(1)} %get-tuple-element.7), channel_id=1, source_target_pairs={{4,0},{8,4},{12,8},{16,12},{20,16},{24,20},{28,24},{0,28},{5,1},{9... | collective-permute-start | bytes 49160 | tf_op jit(solution)/shard_map/ppermute | solution.py:361
  15.2 4.5 %copy-start.6 = (bf16[256,128]{1,0:T(8,128)(2,1)S(1)}, bf16[256,128]{1,0:T(8,128)(2,1)}, u32[]{:S(2)}) copy-start(bf16[256,128]{1,0:T(8,128)(2,1)} %constant.51.clone.1) | copy-start | bytes 196612
  15.2 11.7 %copy-start.12 = (f32[2,64]{1,0:T(2,128)S(1)}, f32[2,64]{1,0:T(2,128)}, u32[]{:S(2)}) copy-start(f32[2,64]{1,0:T(2,128)} %param.17) | copy-start | bytes 1540
  15.2 11.7 %copy-start.13 = (f32[2,64]{1,0:T(2,128)S(1)}, f32[2,64]{1,0:T(2,128)}, u32[]{:S(2)}) copy-start(f32[2,64]{1,0:T(2,128)} %param.19) | copy-start | bytes 1540
  15.2 12.4 %copy-start.1 = (bf16[9,64,128]{2,1,0:T(8,128)(2,1)S(1)}, bf16[9,64,128]{2,1,0:T(8,128)(2,1)}, u32[]{:S(2)}) copy-start(bf16[9,64,128]{2,1,0:T(8,128)(2,1)} %param.20) | copy-start | bytes 442372
  15.2 13.1 %copy-start.14 = (f32[128]{0:T(128)S(1)}, f32[128]{0:T(128)}, u32[]{:S(2)}) copy-start(f32[128]{0:T(128)} %param.21) | copy-start | bytes 1540
  18.0 11.1 %copy-start = (bf16[2,9,64,64]{3,2,1,0:T(8,128)(2,1)S(1)}, bf16[2,9,64,64]{3,2,1,0:T(8,128)(2,1)}, u32[]{:S(2)}) copy-start(bf16[2,9,64,64]{3,2,1,0:T(8,128)(2,1)} %param.18) | copy-start | bytes 442372
  20.4 9.7 %copy-start.9 = (bf16[32,2,128]{2,1,0:T(2,128)(2,1)}, bf16[32,2,128]{2,1,0:T(2,128)(2,1)S(1)}, u32[]{:S(2)}) copy-start(bf16[32,2,128]{2,1,0:T(2,128)(2,1)S(1)} %collective-permute-done.refs_2_) | copy-start | bytes 49156
  20.4 9.7 %copy-start.10 = (bf16[32,2,128]{2,1,0:T(2,128)(2,1)}, bf16[32,2,128]{2,1,0:T(2,128)(2,1)S(1)}, u32[]{:S(2)}) copy-start(bf16[32,2,128]{2,1,0:T(2,128)(2,1)S(1)} %collective-permute-done.1.refs_3_) | copy-start | bytes 49156
  20.5 9.6 %collective-permute-start.3 = (bf16[2,260,128]{2,1,0:T(8,128)(2,1)S(1)}, bf16[2,260,128]{2,1,0:T(8,128)(2,1)S(1)}, u32[]{:S(2)}, u32[]{:S(2)}) collective-permute-start(bf16[2,260,128]{2,1,0:T(8,128)(2,1)S(1)} %pad_maximum_fusion.1), channel_id=1, source_target_pairs={{1,0},{2,1},{3,2},{5,4},{6,5},{7,6},{9,8},{10,9},{11,10},{13,12},{... | collective-permute-start | bytes 399368 | tf_op jit(solution)/shard_map/ppermute | solution.py:361
  21.9 8.2 %collective-permute-start.2 = (bf16[2,260,128]{2,1,0:T(8,128)(2,1)S(1)}, bf16[2,260,128]{2,1,0:T(8,128)(2,1)S(1)}, u32[]{:S(2)}, u32[]{:S(2)}) collective-permute-start(bf16[2,260,128]{2,1,0:T(8,128)(2,1)S(1)} %pad_maximum_fusion), channel_id=1, source_target_pairs={{0,1},{1,2},{2,3},{4,5},{5,6},{6,7},{8,9},{9,10},{10,11},{12,13},{... | collective-permute-start | bytes 399368 | tf_op jit(solution)/shard_map/ppermute | solution.py:360
  30.1 0.7 copy-start.2
  30.1 0.7 copy-start.3
